TPU v7x, 32 devices: a whole 2x2x4 slice. The times are simulated.
32 devices in a mesh: expert: 8 (over z, x), tensor: 4 (over y, core).
Axes of the slice: x: 2, y: 2, z: 4, core: 2. Of those that a mesh axis runs over, the one named last changes fastest.
Arguments:
- inputs: bfloat16 [16384, 768], P(('expert', 'tensor')), may hold values from -6 to 6
- lengths: int32 [16], P('expert'), may hold values from 512 to 1024, as said below
- routes: int32 [16384, 2], P(('expert', 'tensor')), may hold values from 0 to 7, all different within a row; in each aligned block of 512 rows (0 to 511, 512 to 1023, ...) at most 256 rows name the same one
- attn_gain: float32 [768], replicated, may hold values from 0.25 to 1.75
- qkv_weight: bfloat16 [768, 3, 768], P(None, None, 'tensor'), may hold values from -0.21875 to 0.21875
- out_weight: bfloat16 [768, 768], P('tensor'), may hold values from -1.5 to 1.5
- rel_bias: float32 [32, 12], P(None, 'tensor'), may hold values from -4 to 4
- moe_gain: float32 [768], replicated, may hold values from 0.25 to 1.75
- router_weight: bfloat16 [768, 8], replicated, may hold values from -0.15625 to 0.15625
- up_weight: bfloat16 [8, 768, 3072], P('expert', None, 'tensor'), may hold values from -0.21875 to 0.21875
- down_weight: bfloat16 [8, 3072, 768], P('expert', 'tensor'), may hold values from -0.109375 to 0.109375
- out_grad: bfloat16 [16384, 768], P(('expert', 'tensor')), may hold values from -6 to 6
Outputs:
- outputs: bfloat16 [16384, 768], P(('expert', 'tensor'))
- grad_inputs: bfloat16 [16384, 768], P(('expert', 'tensor'))
- grad_attn_gain: float32 [768], replicated
- grad_qkv_weight: float32 [768, 3, 768], P(None, None, 'tensor')
- grad_out_weight: float32 [768, 768], P('tensor')
- grad_rel_bias: float32 [32, 12], P(None, 'tensor')
- grad_moe_gain: float32 [768], replicated
- grad_router: float32 [768, 8], replicated
- grad_up: float32 [8, 768, 3072], P('expert', None, 'tensor')
- grad_down: float32 [8, 3072, 768], P('expert', 'tensor')
Inputs may be any that keep to these rules, and one draw needn't show every extreme that they name: `lengths`: each sequence's real tokens come first, the rest of its 1024 slots are padding; some sequence fills all 1024 slots. `routes`: A token names two different experts. Among the rows of one device no expert is named more than 256 times, and in every draw some device names some expert exactly 256 times.
All inputs are finite; a program needn't handle non-finite values.
Results may differ from a plain program's by a relative error of at most 0.017.
Values may be sent and summed in bfloat16 or wider, within the bound.
A program may use at most 192 MiB of HBM per device.

v0:
```python
import functools

import jax
import jax.numpy as jnp
from jax import lax
from jax.experimental import pallas as pl
from jax.experimental.pallas import tpu as pltpu
from jax.sharding import PartitionSpec as P

D = 768
HD = 64
NB = 32
MAXDIST = 128
SEQ = 1024
EPSILON = 1e-06
NEGATIVE = -1e30
TILE = 256
BF = jnp.bfloat16
F32 = jnp.float32
MIB = 2**20
CHUNK = 256
GELU = 0.7978845608028654
CUBIC = 0.044715


def bucket_edges():
    half_count = NB // 2
    short_edges = list(range(1, half_count))
    long_edges = [
        int(half_count * (MAXDIST / half_count) ** (step_index / half_count))
        for step_index in range(half_count)
    ]
    return short_edges + long_edges


EDGES = bucket_edges()


def dot(a, b, ca=1, cb=0, precision=None):
    return lax.dot_general(
        a, b, (((ca,), (cb,)), ((), ())), preferred_element_type=F32, precision=precision
    )


def iota(shape, dim):
    return lax.broadcasted_iota(jnp.int32, shape, dim)


def rms(v):
    return lax.rsqrt(jnp.mean(v * v, axis=-1, keepdims=True) + EPSILON)


def call(kernel, outs, args, specs=None, scratch=(), flops=0, moved=0, exps=0, vmem=56, name=None):
    vm = pl.BlockSpec(memory_space=pltpu.VMEM)
    return pl.pallas_call(
        kernel,
        out_shape=[jax.ShapeDtypeStruct(s, d) for s, d in outs],
        in_specs=specs or [vm] * len(args),
        out_specs=[vm] * len(outs),
        scratch_shapes=list(scratch),
        compiler_params=pltpu.CompilerParams(vmem_limit_bytes=vmem * MIB),
        cost_estimate=pl.CostEstimate(flops=flops, bytes_accessed=moved, transcendentals=exps),
        name=name,
    )(*args)


VM = pl.BlockSpec(memory_space=pltpu.VMEM)
SM = pl.BlockSpec(memory_space=pltpu.SMEM)


def route_kernel(experts, cap, nv_ref, routes_ref, grad_ref, packed_ref, slots_ref):
    rows = grad_ref.shape[0]
    routes = routes_ref[...]
    first, second = routes[0:1], routes[1:2]
    valid = iota((1, rows), 1) < nv_ref[0]
    ids = iota((experts, rows), 0)
    hot0 = ((ids == first) & valid).astype(F32)
    hot1 = ((ids == second) & valid).astype(F32)
    before = (iota((rows, rows), 0) < iota((rows, rows), 1)).astype(BF)
    rank = dot((hot0 + hot1).astype(BF), before)
    place = ids.astype(F32) * cap + rank
    bad = jnp.where(valid, 0.0, 1.0)
    slot0 = jnp.sum(hot0 * place, axis=0, keepdims=True) - bad
    slot1 = jnp.sum(hot1 * place, axis=0, keepdims=True) - bad
    spots = iota((experts * cap, rows), 0)
    pick0 = spots == slot0.astype(jnp.int32)
    pick1 = spots == slot1.astype(jnp.int32)
    packed_ref[...] = dot((pick0 | pick1).astype(BF), grad_ref[...]).astype(BF)
    slots_ref[...] = jnp.concatenate([slot0, slot1, jnp.zeros((6, rows), F32)], axis=0)


def pick_matrix(slots_ref, spots):
    rows = slots_ref.shape[1]
    where = iota((spots, rows), 0)
    slots = slots_ref[...].astype(jnp.int32)
    return ((where == slots[0:1]) | (where == slots[1:2])).astype(BF)


def back_matrix(slots_ref, spots):
    rows = slots_ref.shape[1]
    where = iota((rows, spots), 1)
    slots = slots_ref[...].T.astype(jnp.int32)
    return ((where == slots[:, 0:1]) | (where == slots[:, 1:2])).astype(BF)


def bias_tiles(table_ref, head):
    dist = iota((8, TILE), 1)
    far = table_ref[NB - 1, head]
    curve = jnp.full((8, TILE), table_ref[0, head] - far, F32)
    for number, edge in enumerate(EDGES):
        curve = jnp.where(dist >= edge, table_ref[number + 1, head] - far, curve)
    spread = jnp.broadcast_to(curve[0:1], (TILE, TILE))
    ring = pltpu.roll(spread, 0, 1, stride=1, stride_axis=0)
    ahead = iota((TILE, TILE), 1) >= iota((TILE, TILE), 0)
    return jnp.where(ahead, ring, NEGATIVE), jnp.where(ahead, 0.0, ring)


def head_pieces(qkvt_ref, mask_rows, head, local_inner):
    start = pl.multiple_of(head * HD, HD)
    q = qkvt_ref[pl.ds(start, HD), :] * jnp.asarray(HD**-0.5, BF)
    k = qkvt_ref[pl.ds(local_inner + start, HD), :]
    v = qkvt_ref[pl.ds(2 * local_inner + start, HD), :]
    ones = jnp.ones((16, SEQ), BF)
    return jnp.concatenate([q, ones], 0), jnp.concatenate([k, mask_rows], 0), v, ones


def mask_block(length):
    keep = (iota((16, SEQ), 1) < length) | (iota((16, SEQ), 0) > 0)
    return jnp.where(keep, 0.0, NEGATIVE).astype(BF)


def score_pieces(k, q, block, near, below):
    cols = slice(block * TILE, (block + 1) * TILE)
    qb = q[:, cols]
    pieces = []
    if block >= 2:
        pieces.append((0, (block - 1) * TILE, dot(k[: (block - 1) * TILE], qb)))
    if block >= 1:
        lo = (block - 1) * TILE
        pieces.append((lo, block * TILE, dot(k[lo : lo + TILE], qb) + below))
    lo = block * TILE
    pieces.append((lo, lo + TILE, dot(k[lo : lo + TILE], qb) + near))
    return cols, pieces


def attn_fwd_kernel(first, heads, scal_ref, table_ref, *refs):
    if first:
        own_ref, other_ref, gain_ref, w_ref, ow_ref = refs[:5]
        normed_ref, qkvt_ref, mixt_ref, lse_ref, part_ref = refs[5:]
        half = own_ref.shape[0]
        core = scal_ref[0]
        for source, place in ((own_ref, core), (other_ref, 1 - core)):
            x = source[...].astype(F32)
            normed_ref[pl.ds(pl.multiple_of(place * half, half), half), :] = (
                x * rms(x) * gain_ref[...]
            ).astype(BF)
    else:
        normed_ref, w_ref, ow_ref, part_in = refs[:4]
        qkvt_ref, mixt_ref, lse_ref, keep_ref, send_ref, part_ref = refs[4:]
    local_inner = heads * HD
    qkvt_ref[...] = dot(w_ref[...], normed_ref[...], 1, 1).astype(BF)
    masks = mask_block(scal_ref[1])
    lse_ref[...] = jnp.zeros_like(lse_ref)

    for head in range(heads):
        near, below = bias_tiles(table_ref, head)
        q, kt, v, ones = head_pieces(qkvt_ref, masks, head, local_inner)
        k = kt.T
        vx = jnp.concatenate([v, ones], 0)
        for block in range(SEQ // TILE):
            cols, pieces = score_pieces(k, q, block, near, below)
            top = functools.reduce(
                jnp.maximum, [jnp.max(s, axis=0, keepdims=True) for _, _, s in pieces]
            )
            total = None
            for lo, hi, s in pieces:
                term = dot(vx[:, lo:hi], jnp.exp(s - top).astype(BF))
                total = term if total is None else total + term
            weight = total[HD : HD + 1]
            mixt_ref[head * HD : (head + 1) * HD, cols] = (total[:HD] / weight).astype(BF)
            lse_ref[head : head + 1, cols] = top + jnp.log(weight)
    part = dot(mixt_ref[...], ow_ref[...], 0, 0)
    if first:
        part_ref[...] = part
    else:
        part_ref[...] = part + part_in[...]
        half = keep_ref.shape[0]
        core = scal_ref[0]
        keep_ref[...] = part_ref[pl.ds(pl.multiple_of(core * half, half), half), :]
        send_ref[...] = part_ref[pl.ds(pl.multiple_of((1 - core) * half, half), half), :].astype(BF)


def attn_bwd_kernel(last, heads, scal_ref, table_ref, *refs):
    if last:
        (normed_ref, w_ref, ow_ref, qkvt_ref, mixt_ref, lse_ref, own_ref, other_ref, part_in) = refs[:9]
        gw_ref, gow_ref, gbias_ref, keep_ref, send_ref, ga_ref, got_ref, gt_ref, d0_ref, d1_ref, part_ref = refs[9:]
    else:
        (normed_ref, w_ref, ow_ref, qkvt_ref, mixt_ref, lse_ref, own_ref, other_ref) = refs[:8]
        gw_ref, gow_ref, gbias_ref, part_ref, ga_ref, got_ref, gt_ref, d0_ref, d1_ref = refs[8:]
    local_inner = heads * HD
    half = own_ref.shape[0]
    core = scal_ref[0]
    ga_ref[pl.ds(pl.multiple_of(core * half, half), half), :] = own_ref[...]
    ga_ref[pl.ds(pl.multiple_of((1 - core) * half, half), half), :] = other_ref[...]
    got_ref[...] = dot(ow_ref[...], ga_ref[...], 1, 1).astype(BF)
    gow_ref[...] = dot(mixt_ref[...], ga_ref[...]).astype(gow_ref.dtype)
    masks = mask_block(scal_ref[1])
    gbias_ref[...] = jnp.zeros_like(gbias_ref)
    ahead = iota((TILE, TILE), 1) >= iota((TILE, TILE), 0)
    spot = (iota((TILE, 128), 0) + 1) % TILE
    flip = (iota((TILE, TILE), 0) + iota((TILE, TILE), 1) == TILE - 1).astype(F32)
    bucket = jnp.zeros((TILE, 128), jnp.int32)
    for edge in EDGES:
        bucket = bucket + (spot >= edge).astype(jnp.int32)
    hot = (bucket == iota((TILE, 128), 1)).astype(F32)

    for head in range(heads):
        near, below = bias_tiles(table_ref, head)
        q, kt, vt, _ = head_pieces(qkvt_ref, masks, head, local_inner)
        k = kt.T
        v = vt.T
        rows = slice(head * HD, (head + 1) * HD)
        gt = got_ref[rows, :]
        delta = jnp.sum(gt.astype(F32) * mixt_ref[rows, :].astype(F32), axis=0, keepdims=True)
        gk = [None] * (SEQ // TILE)
        gv = [None] * (SEQ // TILE)
        far = jnp.zeros((8, TILE), F32)
        for block in range(SEQ // TILE):
            cols, pieces = score_pieces(k, q, block, near, below)
            gb = gt[:, cols]
            qb = q[:HD, cols]
            lse = lse_ref[head : head + 1, cols]
            db = delta[:, cols]
            gq = None
            for lo, hi, s in pieces:
                p = jnp.exp(s - lse)
                ds = p * (dot(v[lo:hi], gb) - db)
                pb = p.astype(BF)
                dsb = ds.astype(BF)
                term = dot(kt[:HD, lo:hi], dsb)
                gq = term if gq is None else gq + term
                tv = dot(pb, gb, 1, 1)
                tk = dot(dsb, qb, 1, 1)
                for tile in range(lo // TILE, hi // TILE):
                    part = slice(tile * TILE - lo, (tile + 1) * TILE - lo)
                    gv[tile] = tv[part] if gv[tile] is None else gv[tile] + tv[part]
                    gk[tile] = tk[part] if gk[tile] is None else gk[tile] + tk[part]
                if hi == (block + 1) * TILE:
                    d0_ref[...] = ds if block == 0 else d0_ref[...] + ds
                elif hi == block * TILE and lo == (block - 1) * TILE:
                    d1_ref[...] = ds if block == 1 else d1_ref[...] + ds
                else:
                    far = far + jnp.sum(ds.reshape((hi - lo) // 8, 8, TILE), axis=0)
            gt_ref[rows, cols] = (gq * HD**-0.5).astype(BF)
        for tile in range(SEQ // TILE):
            cols = slice(tile * TILE, (tile + 1) * TILE)
            gt_ref[local_inner + head * HD : local_inner + (head + 1) * HD, cols] = (
                gk[tile].T.astype(BF)
            )
            gt_ref[2 * local_inner + head * HD : 2 * local_inner + (head + 1) * HD, cols] = (
                gv[tile].T.astype(BF)
            )
        d1 = d1_ref[...]
        ring = jnp.where(ahead, d0_ref[...], d1)
        turned = pltpu.roll(
            dot(flip, ring, 1, 0, lax.Precision.HIGHEST), 0, 1, stride=1, stride_axis=0
        )
        far = far + jnp.sum(jnp.where(ahead, d1, 0.0).reshape(TILE // 8, 8, TILE), axis=0)
        line = jnp.sum(turned, axis=0, keepdims=True)
        sums = dot(
            jnp.broadcast_to(line, (8, TILE)), hot, 1, 0, lax.Precision.HIGHEST
        )
        sums = sums + jnp.where(iota((8, 128), 1) == NB - 1, jnp.sum(far), 0.0)
        gbias_ref[head : head + 1, :] = sums[0:1]
    gw_ref[...] = dot(gt_ref[...], normed_ref[...]).astype(gw_ref.dtype)
    part = dot(gt_ref[...], w_ref[...], 0, 0)
    if last:
        part_ref[...] = part + part_in[...]
        keep_ref[...] = part_ref[pl.ds(pl.multiple_of(core * half, half), half), :]
        send_ref[...] = part_ref[pl.ds(pl.multiple_of((1 - core) * half, half), half), :].astype(BF)
    else:
        part_ref[...] = part


def middle_kernel(
    experts, cap, x_ref, keep_ref, got_ref, gain_ref, router_ref, routes_ref, slots_ref, hidden_ref, packed_ref, meta_ref
):
    hidden = x_ref[...].astype(F32) + keep_ref[...] + got_ref[...].astype(F32)
    hidden_ref[...] = hidden
    normed = (hidden * rms(hidden) * gain_ref[...]).astype(BF)
    rows = hidden.shape[0]
    spots = experts * cap
    slots = slots_ref[...].astype(jnp.int32)
    where = iota((spots, rows), 0)
    pick0 = where == slots[0:1]
    pick1 = where == slots[1:2]
    packed_ref[...] = dot((pick0 | pick1).astype(BF), normed).astype(BF)
    logits = dot(router_ref[...], normed, 1, 1)
    routes = routes_ref[...]
    first, second = routes[0:1], routes[1:2]
    ids = iota((experts, rows), 0)
    gap = jnp.sum(
        logits * ((ids == first).astype(F32) - (ids == second).astype(F32)), axis=0, keepdims=True
    )
    gate0 = 1.0 / (1.0 + jnp.exp(-gap))
    gate1 = 1.0 / (1.0 + jnp.exp(gap))
    line = iota((8, rows), 0)

    def lines(gate, code):
        high = gate.astype(BF).astype(F32)
        mid = (gate - high).astype(BF).astype(F32)
        low = gate - high - mid
        picked = jnp.where(line == 0, high, jnp.where(line == 1, mid, jnp.where(line == 2, low, 0.0)))
        return jnp.where(line == 3, (code + 1).astype(F32), picked).astype(BF)

    meta = dot(lines(gate0, second), pick0.astype(BF), 1, 1) + dot(
        lines(gate1, first), pick1.astype(BF), 1, 1
    )
    for number in range(experts):
        meta_ref[number] = meta[:, number * cap : (number + 1) * cap]


def gelu_pair(v):
    squared = v * v
    slope = GELU * (1.0 + 3 * CUBIC * squared)
    t = jnp.tanh(v * (GELU + GELU * CUBIC * squared))
    half = 0.5 + 0.5 * t
    return v * half, half + 0.5 * v * (1.0 - t * t) * slope


def expert_kernel(
    count, cap, packed_ref, send_meta_ref, grads_ref, router_ref, w0, w1, w2, w3,
    came_ref, result_ref, gw_ref, grouter_ref,
    w_ref, x_ref, xt_ref, geot_ref, act_ref, gi_ref, gsend_ref, meta_ref, acc_ref, stage_ref,
    x_send, x_recv, m_send, m_recv, r_send, r_recv, local_sem, w_sem, out_sem,
):
    me = lax.axis_index("expert")
    barrier = pltpu.get_barrier_semaphore()

    def peer(k):
        return lax.rem(me + k, count)

    def source(k):
        return lax.rem(me + count - k, count)

    def greet(k, carry):
        pl.semaphore_signal(
            barrier, inc=1, device_id={"expert": peer(k)}, device_id_type=pl.DeviceIdType.MESH
        )
        return carry

    lax.fori_loop(1, count, greet, 0)
    pl.semaphore_wait(barrier, count - 1)

    def rows_of(k):
        return pl.ds(pl.multiple_of(k * cap, cap), cap)

    def send_rows(k):
        return pltpu.make_async_remote_copy(
            src_ref=packed_ref.at[rows_of(peer(k))],
            dst_ref=x_ref.at[rows_of(k)],
            send_sem=x_send.at[k],
            recv_sem=x_recv.at[k],
            device_id={"expert": peer(k)},
            device_id_type=pl.DeviceIdType.MESH,
        )

    def send_meta(k):
        return pltpu.make_async_remote_copy(
            src_ref=send_meta_ref.at[peer(k)],
            dst_ref=meta_ref.at[k],
            send_sem=m_send.at[k],
            recv_sem=m_recv.at[k],
            device_id={"expert": peer(k)},
            device_id_type=pl.DeviceIdType.MESH,
        )

    def send_back(k):
        return pltpu.make_async_remote_copy(
            src_ref=gsend_ref.at[rows_of(k)],
            dst_ref=came_ref.at[rows_of(me)],
            send_sem=r_send.at[k],
            recv_sem=r_recv.at[k],
            device_id={"expert": source(k)},
            device_id_type=pl.DeviceIdType.MESH,
        )

    def start_sends(k, carry):
        send_meta(k).start()
        send_rows(k).start()
        return carry

    lax.fori_loop(1, count, start_sends, 0)
    own_rows = pltpu.make_async_copy(packed_ref.at[rows_of(me)], x_ref.at[rows_of(0)], local_sem.at[0])
    own_rows.start()
    own_meta = pltpu.make_async_copy(send_meta_ref.at[me], meta_ref.at[0], local_sem.at[1])
    own_meta.start()
    loads = [
        pltpu.make_async_copy(w, w_ref.at[i], w_sem.at[i]) for i, w in enumerate((w0, w1, w2, w3))
    ]
    for load in loads:
        load.start()
    grouter_ref[...] = jnp.zeros_like(grouter_ref)
    experts = router_ref.shape[1]
    own_rows.wait()
    own_meta.wait()
    for load in loads:
        load.wait()
    group = max(1, CHUNK // cap)
    span = group * cap

    def chunk(j, carry):
        for i in range(group):
            k = j * group + i

            @pl.when(k > 0)
            def _():
                send_rows(k).wait_recv()
                send_meta(k).wait_recv()

        here = pl.ds(pl.multiple_of(j * span, span), span)
        meta = jnp.concatenate([meta_ref[j * group + i].T for i in range(group)], axis=0)
        gate = meta[:, 0:1] + meta[:, 1:2] + meta[:, 2:3]
        code = meta[:, 3:4].astype(jnp.int32)
        gy = jnp.concatenate([grads_ref[rows_of(source(j * group + i)), :] for i in range(group)], axis=0)
        geo = (gate * gy.astype(F32)).astype(BF)
        x = x_ref[here, :]
        xt = x.T
        xt_ref[j] = xt
        geot_ref[j] = geo.T
        acc_ref[...] = jnp.zeros_like(acc_ref)

        def quarter(q, worth):
            inner = dot(x, w_ref[q, :D])
            grad_active = dot(geo, w_ref[q, D:], 1, 1)
            act, slope = gelu_pair(inner)
            gi = (slope * grad_active).astype(BF)
            act_ref[q, here] = act.astype(BF)
            gi_ref[q, here] = gi
            acc_ref[...] += dot(gi, w_ref[q, :D], 1, 1)
            return worth + jnp.sum(act * grad_active, axis=1, keepdims=True)

        worth = lax.fori_loop(0, 4, quarter, jnp.zeros((span, 1), F32))
        ids = iota((span, experts), 1)
        signs = (ids == me).astype(F32) - (ids + 1 == code).astype(F32)
        share = jnp.where(code > 0, (1.0 - gate) * worth, 0.0) * signs
        high = share.astype(BF)
        low = (share - high.astype(F32)).astype(BF)
        gsend_ref[here, :] = (acc_ref[...] + dot(high, router_ref[...], 1, 1)).astype(BF)
        grouter_ref[...] += dot(high.T, x) + dot(low.T, x)
        for i in range(group):
            k = j * group + i

            @pl.when(k > 0)
            def _():
                send_back(k).start()

        return carry

    lax.fori_loop(0, count // group, chunk, 0)
    own_back = pltpu.make_async_copy(gsend_ref.at[rows_of(0)], came_ref.at[rows_of(me)], local_sem.at[0])
    own_back.start()

    def results(j, carry):
        here = pl.ds(pl.multiple_of(j * span, span), span)
        meta = jnp.concatenate([meta_ref[j * group + i].T for i in range(group)], axis=0)
        gate = meta[:, 0:1] + meta[:, 1:2] + meta[:, 2:3]
        acc_ref[...] = jnp.zeros_like(acc_ref)

        def quarter(q, c):
            acc_ref[...] += dot(act_ref[q, here], w_ref[q, D:])
            return c

        lax.fori_loop(0, 4, quarter, 0)
        out = (gate * acc_ref[...]).astype(BF)
        for i in range(group):
            result_ref[rows_of(source(j * group + i)), :] = out[i * cap : (i + 1) * cap]
        return carry

    lax.fori_loop(0, count // group, results, 0)

    tiles = D // TILE

    def store(step, slot):
        q = step // (2 * tiles)
        place = lax.rem(step, 2 * tiles)
        return pltpu.make_async_copy(
            stage_ref.at[slot],
            gw_ref.at[q, pl.ds(pl.multiple_of(place * TILE, TILE), TILE)],
            out_sem.at[slot],
        )

    def weights(step, carry):
        q = step // (2 * tiles)
        place = lax.rem(step, 2 * tiles)
        slot = lax.rem(step, 2)

        @pl.when(step >= 2)
        def _():
            store(step - 2, slot).wait()

        def reduce(left_ref, right_ref, tile):
            acc_ref[...] = jnp.zeros_like(acc_ref)

            def one(j, c):
                lines = pl.ds(pl.multiple_of(tile * TILE, TILE), TILE)
                there = pl.ds(pl.multiple_of(j * span, span), span)
                acc_ref[...] += dot(left_ref[j, lines], right_ref[q, there])
                return c

            lax.fori_loop(0, count // group, one, 0)
            stage_ref[slot] = acc_ref[...].astype(BF)

        @pl.when(place < tiles)
        def _():
            reduce(xt_ref, gi_ref, place)

        @pl.when(place >= tiles)
        def _():
            reduce(geot_ref, act_ref, place - tiles)

        store(step, slot).start()
        return carry

    steps = 8 * tiles
    lax.fori_loop(0, steps, weights, 0)
    for step in (steps - 2, steps - 1):
        store(step, step % 2).wait()
    own_back.wait()

    def finish(k, carry):
        send_rows(k).wait_send()
        send_meta(k).wait_send()
        send_back(k).wait()
        return carry

    lax.fori_loop(1, count, finish, 0)


def turn_kernel(nv_ref, came_ref, slots_ref, hidden_ref, gain_ref, grad_ref, gh_ref, ga_ref, gain_out):
    gn = dot(back_matrix(slots_ref, came_ref.shape[0]), came_ref[...])
    hidden = hidden_ref[...]
    scale = rms(hidden)
    unit = hidden * scale
    gain_out[...] = jnp.broadcast_to(jnp.sum(gn * unit, axis=0, keepdims=True), gain_out.shape)
    g = gn * gain_ref[...]
    valid = (iota((hidden.shape[0], 1), 0) < nv_ref[0]).astype(F32)
    gh = scale * (g - unit * jnp.mean(g * unit, axis=1, keepdims=True)) + valid * grad_ref[...].astype(F32)
    gh_ref[...] = gh
    ga_ref[...] = gh.astype(BF)


def output_kernel(nv_ref, came_ref, slots_ref, hidden_ref, out_ref):
    mix = dot(back_matrix(slots_ref, came_ref.shape[0]), came_ref[...])
    hidden = hidden_ref[...]
    valid = (iota((hidden.shape[0], 1), 0) < nv_ref[0]).astype(F32)
    out_ref[...] = (valid * (hidden + mix)).astype(BF)


def last_kernel(x_ref, keep_ref, got_ref, gain_ref, gh_ref, out_ref, gain_out):
    x = x_ref[...].astype(F32)
    scale = rms(x)
    unit = x * scale
    gn = keep_ref[...] + got_ref[...].astype(F32)
    gain_out[...] = jnp.broadcast_to(jnp.sum(gn * unit, axis=0, keepdims=True), gain_out.shape)
    g = gn * gain_ref[...]
    out_ref[...] = (
        gh_ref[...] + scale * (g - unit * jnp.mean(g * unit, axis=1, keepdims=True))
    ).astype(BF)


def moe(experts, cap, packed, meta, grads, router, quarters):
    spots = experts * cap
    groups = spots // CHUNK
    anyspec = pl.BlockSpec(memory_space=pl.ANY)
    dma = pltpu.SemaphoreType.DMA
    return pl.pallas_call(
        functools.partial(expert_kernel, experts, cap),
        out_shape=[
            jax.ShapeDtypeStruct((spots, D), BF),
            jax.ShapeDtypeStruct((spots, D), BF),
            jax.ShapeDtypeStruct((4, 2 * D, D), BF),
            jax.ShapeDtypeStruct((experts, D), F32),
        ],
        in_specs=[anyspec, VM, VM, VM] + [anyspec] * 4,
        out_specs=[anyspec, VM, anyspec, VM],
        scratch_shapes=[
            pltpu.VMEM((4, 2 * D, D), BF),
            pltpu.VMEM((spots, D), BF),
            pltpu.VMEM((groups, D, CHUNK), BF),
            pltpu.VMEM((groups, D, CHUNK), BF),
            pltpu.VMEM((4, spots, D), BF),
            pltpu.VMEM((4, spots, D), BF),
            pltpu.VMEM((spots, D), BF),
            pltpu.VMEM((experts, 8, cap), F32),
            pltpu.VMEM((CHUNK, D), F32),
            pltpu.VMEM((2, CHUNK, D), BF),
            dma((experts,)),
            dma((experts,)),
            dma((experts,)),
            dma((experts,)),
            dma((experts,)),
            dma((experts,)),
            dma((2,)),
            dma((4,)),
            dma((2,)),
        ],
        compiler_params=pltpu.CompilerParams(
            collective_id=1, has_side_effects=True, vmem_limit_bytes=60 * MIB
        ),
        cost_estimate=pl.CostEstimate(flops=12 * spots * D * 4 * D, bytes_accessed=60 * MIB, transcendentals=0),
        name="experts",
    )(packed, meta, grads, router, *quarters)


def shards(
    inputs,
    lengths,
    routes,
    attn_gain,
    qkv_weight,
    out_weight,
    rel_bias,
    moe_gain,
    router_weight,
    up_weight,
    down_weight,
    out_grad,
):
    rows = inputs.shape[0]
    rank = lax.axis_index("tensor")
    expert = lax.axis_index("expert")
    heads = rel_bias.shape[1]
    inner = heads * HD
    experts = router_weight.shape[1]
    cap = 4 * rows // experts
    spots = experts * cap
    core = rank % 2
    length = lengths[rank // 2]
    nvalid = jnp.clip(length - core * rows, 0, rows).astype(jnp.int32).reshape(1)
    scal = jnp.stack([core, length]).astype(jnp.int32)

    def swap(x, bit):
        return lax.ppermute(x, "tensor", [(i, i ^ bit) for i in range(4)])

    gain1 = attn_gain.reshape(1, D)
    gain2 = moe_gain.reshape(1, D)
    other = swap(inputs, 1)
    wt = jnp.transpose(qkv_weight.reshape(D, 3 * inner))
    pair_w = swap(jnp.concatenate([wt, out_weight], axis=0), 2)
    pair_table = swap(rel_bias, 2)

    routes_t = jnp.transpose(routes)
    packed_grad, slots = call(
        functools.partial(route_kernel, experts, cap),
        [((spots, D), BF), ((8, rows), F32)],
        (nvalid, routes_t, out_grad),
        [SM, VM, VM],
        flops=2 * spots * rows * D,
        moved=4 * MIB,
        name="route",
    )

    def exchange(x):
        return lax.all_to_all(
            x.reshape(experts, cap, x.shape[-1]), "expert", split_axis=0, concat_axis=0, tiled=True
        ).reshape(x.shape)

    grads_in = exchange(packed_grad)
    mine = jnp.concatenate([up_weight[0], down_weight[0]], axis=0)
    far = swap(mine, 2)
    side = swap(mine, 1)
    cross = swap(far, 1)
    quarters = [mine, side, far, cross]

    attn_cost = dict(
        flops=2 * SEQ * D * 4 * inner + heads * SEQ * SEQ * 160, moved=6 * MIB, exps=heads * SEQ * SEQ
    )
    normed, qkvt0, mixt0, lse0, part0 = call(
        functools.partial(attn_fwd_kernel, True, heads),
        [((SEQ, D), BF), ((3 * inner, SEQ), BF), ((inner, SEQ), BF), ((8, SEQ), F32), ((SEQ, D), F32)],
        (scal, rel_bias, inputs, other, gain1, wt, out_weight),
        [SM, SM] + [VM] * 5,
        name="attend_own",
        **attn_cost,
    )
    wt1, ow1 = pair_w[: 3 * inner], pair_w[3 * inner :]
    qkvt1, mixt1, lse1, keep, send = call(
        functools.partial(attn_fwd_kernel, False, heads),
        [((3 * inner, SEQ), BF), ((inner, SEQ), BF), ((8, SEQ), F32), ((rows, D), F32), ((rows, D), BF)],
        (scal, pair_table, normed, wt1, ow1, part0),
        [SM, SM] + [VM] * 4,
        scratch=[pltpu.VMEM((SEQ, D), F32)],
        name="attend_pair",
        **attn_cost,
    )
    got = swap(send, 1)
    hidden, packed_rows, meta = call(
        functools.partial(middle_kernel, experts, cap),
        [((rows, D), F32), ((spots, D), BF), ((experts, 8, cap), F32)],
        (inputs, keep, got, gain2, jnp.transpose(router_weight), routes_t, slots),
        flops=2 * spots * rows * D,
        moved=8 * MIB,
        name="middle",
    )
    came, result, weight_grads, grad_router = moe(
        experts, cap, packed_rows, meta, grads_in, router_weight, quarters
    )
    came_out = exchange(result)

    grads = weight_grads
    near = grads[0].astype(F32) + swap(grads[1], 1).astype(F32)
    away = grads[2].astype(F32) + swap(grads[3], 1).astype(F32)
    grad_weights = near + swap(away.astype(BF), 2).astype(F32)

    grad_hidden, grad_attended, moe_part = call(
        turn_kernel,
        [((rows, D), F32), ((rows, D), BF), ((8, D), F32)],
        (nvalid, came, slots, hidden, gain2, out_grad),
        [SM] + [VM] * 5,
        flops=2 * spots * rows * D,
        moved=8 * MIB,
        name="turn",
    )
    other_grad = swap(grad_attended, 1)
    bwd_cost = dict(
        flops=2 * SEQ * D * 10 * inner + heads * SEQ * SEQ * 400, moved=9 * MIB, exps=heads * SEQ * SEQ
    )
    work = [
        pltpu.VMEM((SEQ, D), BF),
        pltpu.VMEM((inner, SEQ), BF),
        pltpu.VMEM((3 * inner, SEQ), BF),
        pltpu.VMEM((TILE, TILE), F32),
        pltpu.VMEM((TILE, TILE), F32),
    ]
    gw1, gow1, gbias1, npart = call(
        functools.partial(attn_bwd_kernel, False, heads),
        [((3 * inner, D), BF), ((inner, D), BF), ((8, 128), F32), ((SEQ, D), F32)],
        (scal, pair_table, normed, wt1, ow1, qkvt1, mixt1, lse1, grad_attended, other_grad),
        [SM, SM] + [VM] * 8,
        scratch=work,
        name="attend_pair_back",
        **bwd_cost,
    )
    gpair = swap(jnp.concatenate([gw1, gow1], axis=0), 2)
    gw0, gow0, gbias0, keep_n, send_n = call(
        functools.partial(attn_bwd_kernel, True, heads),
        [((3 * inner, D), F32), ((inner, D), F32), ((8, 128), F32), ((rows, D), F32), ((rows, D), BF)],
        (scal, rel_bias, normed, wt, out_weight, qkvt0, mixt0, lse0, grad_attended, other_grad, npart),
        [SM, SM] + [VM] * 9,
        scratch=work + [pltpu.VMEM((SEQ, D), F32)],
        name="attend_own_back",
        **bwd_cost,
    )
    got_n = swap(send_n, 1)
    grad_inputs, attn_part = call(
        last_kernel,
        [((rows, D), BF), ((8, D), F32)],
        (inputs, keep_n, got_n, gain1, grad_hidden),
        moved=6 * MIB,
        name="last",
    )
    wide = (jnp.concatenate([gw0, gow0], axis=0) + gpair.astype(F32)).astype(BF)
    wide = lax.psum(wide, "expert").astype(F32)
    outputs = call(
        output_kernel,
        [((rows, D), BF)],
        (nvalid, came_out, slots, hidden),
        [SM] + [VM] * 3,
        flops=2 * spots * rows * D,
        moved=8 * MIB,
        name="outputs",
    )[0]

    own_bias = gbias0[:heads, :NB].reshape(1, -1)
    pair_bias = gbias1[:heads, :NB].reshape(1, -1)
    ranks = jnp.arange(4, dtype=jnp.int32)[:, None]
    bias_parts = jnp.where(ranks == rank, own_bias, 0.0) + jnp.where(ranks == (rank ^ 2), pair_bias, 0.0)
    small = jnp.concatenate(
        [attn_part[0], moe_part[0], jnp.transpose(grad_router).reshape(-1), bias_parts.reshape(-1)]
    )
    small = lax.psum(small, ("expert", "tensor"))
    bias_sum = lax.dynamic_slice(
        small[2 * D + experts * D :].reshape(4, heads * NB), (rank, 0), (1, heads * NB)
    )
    return (
        outputs,
        grad_inputs,
        small[:D],
        jnp.transpose(wide[: 3 * inner]).reshape(D, 3, inner),
        wide[3 * inner :],
        jnp.transpose(bias_sum.reshape(heads, NB)),
        small[D : 2 * D],
        small[2 * D : 2 * D + experts * D].reshape(D, experts),
        grad_weights[:D][None],
        jnp.transpose(grad_weights[D:])[None],
    )


def solution(mesh):
    return jax.shard_map(
        shards,
        mesh=mesh,
        in_specs=(
            P(("expert", "tensor"), None),
            P("expert"),
            P(("expert", "tensor"), None),
            P(),
            P(None, None, "tensor"),
            P("tensor", None),
            P(None, "tensor"),
            P(),
            P(),
            P("expert", None, "tensor"),
            P("expert", "tensor", None),
            P(("expert", "tensor"), None),
        ),
        out_specs=(
            P(("expert", "tensor"), None),
            P(("expert", "tensor"), None),
            P(),
            P(None, None, "tensor"),
            P("tensor", None),
            P(None, "tensor"),
            P(),
            P(),
            P("expert", None, "tensor"),
            P("expert", "tensor", None),
        ),
        check_vma=False,
    )
```

profile of v0, /device:TPU:0, one launch (start us, length us, event | category | flops | bytes accessed | tf_op | source)
XLA Modules:
  0.0 525.4 jit_solution(13065567147445900369)
XLA Ops:
  9.1 4.8 route.1
  13.9 7.2 %all-to-all-start = ((bf16[8,256,768]{2,1,0:T(8,128)(2,1)}), bf16[8,256,768]{2,1,0:T(8,128)(2,1)S(1)}, u32[]{:S(2)}, u32[]{:S(2)}) async-start(bf16[8,256,768]{2,1,0:T(8,128)(2,1)} %bitcast.36), calls=%async_computation | async-start | bytes 6291456 | tf_op jit(solution)/shard_map/all_to_all | solution.py:665
  21.1 3.3 pad_maximum_fusion.w0
  25.9 51.5 %collective-permute-done.5.w2 = bf16[1536,768]{1,0:T(8,128)(2,1)} collective-permute-done((bf16[1536,768]{1,0:T(8,128)(2,1)}, bf16[1536,768]{1,0:T(8,128)(2,1)}, u32[]{:S(2)}, u32[]{:S(2)}) %collective-permute-start.5) | collective-permute-done | bytes 2359328 | tf_op jit(solution)/shard_map/ppermute | solution.py:644
  83.4 10.0 %attend_own.1 = (bf16[1024,768]{1,0:T(8,128)(2,1)}, bf16[576,1024]{1,0:T(8,128)(2,1)}, bf16[192,1024]{1,0:T(8,128)(2,1)}, f32[8,1024]{1,0:T(8,128)}, f32[1024,768]{1,0:T(8,128)}) custom-call(s32[2]{0:T(128)} %pad_add_fusion.scal_ref, f32[32,3]{1,0:T(8,128)} %copy-done.6, bf16[512,768]{1,0:T(8,128)(2,1)} %x_ref.3, ...), custom_call_target="tpu_custom_call" | custom-call | flops 1711276032 | bytes 6291456 | tf_op jit(solution)/shard_map/attend_own/pallas_call | solution.py:55
  93.5 13.9 %collective-permute-done.2 = bf16[768,768]{1,0:T(8,128)(2,1)} collective-permute-done((bf16[768,768]{1,0:T(8,128)(2,1)}, bf16[768,768]{1,0:T(8,128)(2,1)}, u32[]{:S(2)}, u32[]{:S(2)}) %collective-permute-start.2) | collective-permute-done | bytes 1179680 | tf_op jit(solution)/shard_map/ppermute | solution.py:644
  107.4 2.1 slice.88.refs_1_
  111.9 10.1 %attend_pair.1 = (bf16[576,1024]{1,0:T(8,128)(2,1)}, bf16[192,1024]{1,0:T(8,128)(2,1)}, f32[8,1024]{1,0:T(8,128)}, f32[512,768]{1,0:T(8,128)}, bf16[512,768]{1,0:T(8,128)(2,1)}) custom-call(s32[2]{0:T(128)} %pad_add_fusion.scal_ref, f32[32,3]{1,0:T(8,128)} %copy-done.14, bf16[1024,768]{1,0:T(8,128)(2,1)} %get-tuple-element.43.refs_0_, ...), custom_call_target="tpu_custom_call" | custom-call | flops 1711276032 | bytes 6291456 | tf_op jit(solution)/shard_map/attend_pair/pallas_call | solution.py:55
  124.6 7.3 %middle.1 = (f32[512,768]{1,0:T(8,128)}, bf16[2048,768]{1,0:T(8,128)(2,1)}, f32[8,8,256]{2,1,0:T(8,128)}) custom-call(bf16[512,768]{1,0:T(8,128)(2,1)} %x_ref.3, f32[512,768]{1,0:T(8,128)} %get-tuple-element.45.keep_ref, bf16[512,768]{1,0:T(8,128)(2,1)} %collective-permute-done.3.got_ref, f32[1,768]{1,0:T(1,128)} %reshape.106.gain_ref, ...), custom_call_target="tpu_custom_call" | custom-call | flops 1610612736 | bytes 8388608 | tf_op jit(solution)/shard_map/middle/pallas_call | solution.py:55
  133.6 157.0 %experts.1 = (bf16[2048,768]{1,0:T(8,128)(2,1)}, bf16[2048,768]{1,0:T(8,128)(2,1)}, bf16[4,1536,768]{2,1,0:T(8,128)(2,1)}, f32[8,768]{1,0:T(8,128)}) custom-call(bf16[2048,768]{1,0:T(8,128)(2,1)} %get-tuple-element.48.packed_ref, f32[8,8,256]{2,1,0:T(8,128)} %get-tuple-element.49.send_meta_ref, bf16[2048,768]{1,0:T(8,128)(2,1)} %bitcast.35, ...), custom_call_target="tpu_custom_call" | custom-call | flops 57982058496 | bytes 62914560 | tf_op jit(solution)/shard_map/experts/pallas_call | solution.py:577
  290.7 4.1 slice_bitcast_fusion.3
  294.8 6.8 %turn.1 = (f32[512,768]{1,0:T(8,128)}, bf16[512,768]{1,0:T(8,128)(2,1)}, f32[8,768]{1,0:T(8,128)}) custom-call(s32[1]{0:T(128)} %bitcast.1.nv_ref, bf16[2048,768]{1,0:T(8,128)(2,1)} %get-tuple-element.56.came_ref, f32[8,512]{1,0:T(8,128)} %get-tuple-element.47.slots_ref, f32[512,768]{1,0:T(8,128)} %get-tuple-element.52.hidden_ref, ...), custom_call_target="tpu_custom_call" | custom-call | flops 1610612736 | bytes 8388608 | tf_op jit(solution)/shard_map/turn/pallas_call | solution.py:55
  302.1 57.6 %all-to-all-start.1 = ((bf16[8,256,768]{2,1,0:T(8,128)(2,1)}), bf16[8,256,768]{2,1,0:T(8,128)(2,1)}, u32[]{:S(2)}, u32[]{:S(2)}) async-start(bf16[8,256,768]{2,1,0:T(8,128)(2,1)} %bitcast.12), calls=%async_computation.1 | async-start | bytes 6291456 | tf_op jit(solution)/shard_map/all_to_all | solution.py:665
  360.9 16.3 %attend_pair_back.1 = (bf16[576,768]{1,0:T(8,128)(2,1)}, bf16[192,768]{1,0:T(8,128)(2,1)}, f32[8,128]{1,0:T(8,128)}, f32[1024,768]{1,0:T(8,128)}) custom-call(s32[2]{0:T(128)} %pad_add_fusion.scal_ref, f32[32,3]{1,0:T(8,128)} %copy-done.14, bf16[1024,768]{1,0:T(8,128)(2,1)} %get-tuple-element.43.refs_0_, bf16[576,768]{1,0:T(8,128)(2,1)} %slice.88.refs_1_, ...), custom_call_target="tpu_custom_call" | custom-call | flops 4278190080 | bytes 9437184 | tf_op jit(solution)/shard_map/attend_pair_back/pallas_call | solution.py:55
  380.2 3.0 fusion
  383.7 17.4 %attend_own_back.1 = (f32[576,768]{1,0:T(8,128)}, f32[192,768]{1,0:T(8,128)}, f32[8,128]{1,0:T(8,128)}, f32[512,768]{1,0:T(8,128)}, bf16[512,768]{1,0:T(8,128)(2,1)}) custom-call(s32[2]{0:T(128)} %pad_add_fusion.scal_ref, f32[32,3]{1,0:T(8,128)} %copy-done.6, bf16[1024,768]{1,0:T(8,128)(2,1)} %get-tuple-element.43.refs_0_, bf16[576,768]{1,0:T(8,128)(2,1)} %bitcast.41, ...), custom_call_target="tpu_custom_call" | custom-call | flops 4278190080 | bytes 9437184 | tf_op jit(solution)/shard_map/attend_own_back/pallas_call | solution.py:55
  401.1 6.3 %collective-permute-done.9 = bf16[768,768]{1,0:T(8,128)(2,1)S(1)} collective-permute-done((bf16[768,768]{1,0:T(8,128)(2,1)S(1)}, bf16[768,768]{1,0:T(8,128)(2,1)S(1)}, u32[]{:S(2)}, u32[]{:S(2)}) %collective-permute-start.9) | collective-permute-done | bytes 1179680 | tf_op jit(solution)/shard_map/ppermute | solution.py:644
  407.4 2.9 fusion.2
  414.1 4.1 last.1
  419.0 73.7 %psum.14 = f32[8064]{0:T(1024)S(1)} all-reduce(f32[8064]{0:T(1024)S(1)} %pad_maximum_fusion.3), channel_id=1, replica_groups=mesh['expert'=8,'tensor'=4] {'expert','tensor'}, use_global_device_ids=true, to_apply=%region_0.1 | all-reduce | flops 8064 | bytes 64512 | tf_op jit(solution)/shard_map/psum | solution.py:782
  495.1 6.5 %all-reduce.2.cloned.1.call-done = bf16[768,768]{1,0:T(8,128)(2,1)} async-done(((bf16[768,768]{1,0:T(8,128)(2,1)}), bf16[768,768]{1,0:T(8,128)(2,1)}) %all-reduce.2.cloned.1.call-update) | async-done | bytes 1179664 | tf_op jit(solution)/shard_map/psum | solution.py:764
  501.6 2.6 slice.91
  505.0 3.9 fusion.1
  512.6 5.6 %outputs.1 = bf16[512,768]{1,0:T(8,128)(2,1)} custom-call(s32[1]{0:T(128)} %bitcast.1.nv_ref, bf16[2048,768]{1,0:T(8,128)(2,1)} %bitcast.13.came_ref, f32[8,512]{1,0:T(8,128)} %get-tuple-element.47.slots_ref, f32[512,768]{1,0:T(8,128)} %get-tuple-element.52.hidden_ref), custom_call_target="tpu_custom_call" | custom-call | flops 1610612736 | bytes 8388608 | tf_op jit(solution)/shard_map/outputs/pallas_call | solution.py:55
  (89 shorter events, 31.9 us)
Async XLA Ops:
  13.9 118.1 %all-to-all-start = ((bf16[8,256,768]{2,1,0:T(8,128)(2,1)}), bf16[8,256,768]{2,1,0:T(8,128)(2,1)S(1)}, u32[]{:S(2)}, u32[]{:S(2)}) async-start(bf16[8,256,768]{2,1,0:T(8,128)(2,1)} %bitcast.36), calls=%async_computation | async-start | bytes 6291456 | tf_op jit(solution)/shard_map/all_to_all | solution.py:665
  21.1 56.3 %copy-start.2 = (bf16[768,3,192]{0,2,1:T(8,128)(2,1)S(1)}, bf16[768,3,192]{0,2,1:T(8,128)(2,1)}, u32[]{:S(2)}) copy-start(bf16[768,3,192]{0,2,1:T(8,128)(2,1)} %param.16) | copy-start | bytes 2654212
  21.1 56.3 %copy-start.4 = (bf16[192,768]{1,0:T(8,128)(2,1)S(1)}, bf16[192,768]{1,0:T(8,128)(2,1)}, u32[]{:S(2)}) copy-start(bf16[192,768]{1,0:T(8,128)(2,1)} %refs_2_.1) | copy-start | bytes 884740
  24.4 55.9 %copy-start.10 = (f32[32,3]{0,1:T(4,128)S(1)}, f32[32,3]{0,1:T(4,128)}, u32[]{:S(2)}) copy-start(f32[32,3]{0,1:T(4,128)} %param.18) | copy-start | bytes 1156
  24.4 56.5 %copy-start.8 = (f32[768]{0:T(1024)S(1)}, f32[768]{0:T(1024)}, u32[]{:S(2)}) copy-start(f32[768]{0:T(1024)} %param.15) | copy-start | bytes 9220
  24.4 53.0 %collective-permute-start.5 = (bf16[1536,768]{1,0:T(8,128)(2,1)}, bf16[1536,768]{1,0:T(8,128)(2,1)}, u32[]{:S(2)}, u32[]{:S(2)}) collective-permute-start(bf16[1536,768]{1,0:T(8,128)(2,1)} %pad_maximum_fusion.w0), channel_id=1, source_target_pairs={{0,2},{1,3},{2,0},{3,1},{4,6},{5,7},{6,4},{7,5},{8,10},{9,11},{10,... | collective-permute-start | bytes 7077896 | tf_op jit(solution)/shard_map/ppermute | solution.py:644
  25.9 106.0 %collective-permute-start.4 = (bf16[1536,768]{1,0:T(8,128)(2,1)}, bf16[1536,768]{1,0:T(8,128)(2,1)}, u32[]{:S(2)}, u32[]{:S(2)}) collective-permute-start(bf16[1536,768]{1,0:T(8,128)(2,1)} %pad_maximum_fusion.w0), channel_id=1, source_target_pairs={{0,1},{1,0},{2,3},{3,2},{4,5},{5,4},{6,7},{7,6},{8,9},{9,8},{10,11... | collective-permute-start | bytes 7077896 | tf_op jit(solution)/shard_map/ppermute | solution.py:644
  77.4 54.5 %collective-permute-start.6 = (bf16[1536,768]{1,0:T(8,128)(2,1)}, bf16[1536,768]{1,0:T(8,128)(2,1)}, u32[]{:S(2)}, u32[]{:S(2)}) collective-permute-start(bf16[1536,768]{1,0:T(8,128)(2,1)} %collective-permute-done.5.w2), channel_id=1, source_target_pairs={{0,1},{1,0},{2,3},{3,2},{4,5},{5,4},{6,7},{7,6},{8,9},{9,8},{10,11... | collective-permute-start | bytes 7077896 | tf_op jit(solution)/shard_map/ppermute | solution.py:644
  78.5 28.9 %collective-permute-start.2 = (bf16[768,768]{1,0:T(8,128)(2,1)}, bf16[768,768]{1,0:T(8,128)(2,1)}, u32[]{:S(2)}, u32[]{:S(2)}) collective-permute-start(bf16[768,768]{1,0:T(8,128)(2,1)} %pad_maximum_fusion.1), channel_id=1, source_target_pairs={{0,2},{1,3},{2,0},{3,1},{4,6},{5,7},{6,4},{7,5},{8,10},{9,11},{10,... | collective-permute-start | bytes 3538952 | tf_op jit(solution)/shard_map/ppermute | solution.py:644
  80.1 3.4 collective-permute-start.1
  80.4 30.9 %collective-permute-start = (f32[32,3]{1,0:T(8,128)S(1)}, f32[32,3]{1,0:T(8,128)S(1)}, u32[]{:S(2)}, u32[]{:S(2)}) collective-permute-start(f32[32,3]{1,0:T(8,128)S(1)} %copy.27.table_ref), channel_id=1, source_target_pairs={{0,2},{1,3},{2,0},{3,1},{4,6},{5,7},{6,4},{7,5},{8,10},{9,11},{10,... | collective-permute-start | bytes 1160 | tf_op jit(solution)/shard_map/ppermute | solution.py:644
  111.9 10.1 %copy-start.9 = (f32[768]{0:T(1024)S(1)}, f32[768]{0:T(1024)}, u32[]{:S(2)}) copy-start(f32[768]{0:T(1024)} %param.19) | copy-start | bytes 9220
  111.9 10.7 %copy-start.7 = (bf16[768,8]{0,1:T(8,128)(2,1)S(1)}, bf16[768,8]{0,1:T(8,128)(2,1)}, u32[]{:S(2)}) copy-start(bf16[768,8]{0,1:T(8,128)(2,1)} %param.20) | copy-start | bytes 36868
  122.0 2.6 collective-permute-start.3
  294.7 85.4 %collective-permute-start.11 = (bf16[1536,768]{1,0:T(8,128)(2,1)S(1)}, bf16[1536,768]{1,0:T(8,128)(2,1)}, u32[]{:S(2)}, u32[]{:S(2)}) collective-permute-start(bf16[1536,768]{1,0:T(8,128)(2,1)S(1)} %get-tuple-element.97), channel_id=1, source_target_pairs={{0,1},{1,0},{2,3},{3,2},{4,5},{5,4},{6,7},{7,6},{8,9},{9,8},{10,11... | collective-permute-start | bytes 7077896 | tf_op jit(solution)/shard_map/ppermute | solution.py:644
  301.6 58.4 %collective-permute-start.7 = (bf16[512,768]{1,0:T(8,128)(2,1)}, bf16[512,768]{1,0:T(8,128)(2,1)S(1)}, u32[]{:S(2)}, u32[]{:S(2)}) collective-permute-start(bf16[512,768]{1,0:T(8,128)(2,1)} %get-tuple-element.57.refs_6_), channel_id=1, source_target_pairs={{0,1},{1,0},{2,3},{3,2},{4,5},{5,4},{6,7},{7,6},{8,9},{9,8},{10,11... | collective-permute-start | bytes 2359304 | tf_op jit(solution)/shard_map/ppermute | solution.py:644
  302.1 210.5 %all-to-all-start.1 = ((bf16[8,256,768]{2,1,0:T(8,128)(2,1)}), bf16[8,256,768]{2,1,0:T(8,128)(2,1)}, u32[]{:S(2)}, u32[]{:S(2)}) async-start(bf16[8,256,768]{2,1,0:T(8,128)(2,1)} %bitcast.12), calls=%async_computation.1 | async-start | bytes 6291456 | tf_op jit(solution)/shard_map/all_to_all | solution.py:665
  359.7 141.9 %all-reduce.2.cloned.1.call-start = ((), (), s32[]{:S(2)}) async-start(), calls=%async_computation.2 | async-start | bytes 2359296 | tf_op jit(solution)/shard_map/psum | solution.py:764
  359.9 145.1 %collective-permute-start.10 = (bf16[1536,768]{1,0:T(8,128)(2,1)}, bf16[1536,768]{1,0:T(8,128)(2,1)}, u32[]{:S(2)}, u32[]{:S(2)}) collective-permute-start(bf16[1536,768]{1,0:T(8,128)(2,1)} %get-tuple-element.96), channel_id=1, source_target_pairs={{0,1},{1,0},{2,3},{3,2},{4,5},{5,4},{6,7},{7,6},{8,9},{9,8},{10,11... | collective-permute-start | bytes 7077896 | tf_op jit(solution)/shard_map/ppermute | solution.py:644
  378.6 28.8 %collective-permute-start.9 = (bf16[768,768]{1,0:T(8,128)(2,1)S(1)}, bf16[768,768]{1,0:T(8,128)(2,1)S(1)}, u32[]{:S(2)}, u32[]{:S(2)}) collective-permute-start(bf16[768,768]{1,0:T(8,128)(2,1)S(1)} %pad_maximum_fusion.2), channel_id=1, source_target_pairs={{0,2},{1,3},{2,0},{3,1},{4,6},{5,7},{6,4},{7,5},{8,10},{9,11},{10,... | collective-permute-start | bytes 3538952 | tf_op jit(solution)/shard_map/ppermute | solution.py:644
  383.1 121.9 %collective-permute-start.12 = (bf16[1536,768]{1,0:T(8,128)(2,1)S(1)}, bf16[1536,768]{1,0:T(8,128)(2,1)}, u32[]{:S(2)}, u32[]{:S(2)}) collective-permute-start(bf16[1536,768]{1,0:T(8,128)(2,1)S(1)} %fusion), channel_id=1, source_target_pairs={{0,2},{1,3},{2,0},{3,1},{4,6},{5,7},{6,4},{7,5},{8,10},{9,11},{10,... | collective-permute-start | bytes 7077896 | tf_op jit(solution)/shard_map/ppermute | solution.py:644
  401.1 12.1 %collective-permute-start.8 = (bf16[512,768]{1,0:T(8,128)(2,1)}, bf16[512,768]{1,0:T(8,128)(2,1)S(1)}, u32[]{:S(2)}, u32[]{:S(2)}) collective-permute-start(bf16[512,768]{1,0:T(8,128)(2,1)} %get-tuple-element.63), channel_id=1, source_target_pairs={{0,1},{1,0},{2,3},{3,2},{4,5},{5,4},{6,7},{7,6},{8,9},{9,8},{10,11... | collective-permute-start | bytes 2359304 | tf_op jit(solution)/shard_map/ppermute | solution.py:644
  407.4 5.5 %copy-start.12 = (f32[8,128]{1,0:T(8,128)S(1)}, f32[8,128]{1,0:T(8,128)}, u32[]{:S(2)}) copy-start(f32[8,128]{1,0:T(8,128)} %get-tuple-element.69) | copy-start | bytes 12292
  407.4 5.6 %copy-start.11 = (f32[8,128]{1,0:T(8,128)S(1)}, f32[8,128]{1,0:T(8,128)}, u32[]{:S(2)}) copy-start(f32[8,128]{1,0:T(8,128)} %get-tuple-element.70) | copy-start | bytes 12292
  (7 other events, 14.6 us)
Sparse Core Ops, SparseCore 0:
  410.5 91.0 all-reduce.1
where the time goes:
time: 536 us; the launch traced here: 525 us
  Pallas kernels  239 us (45%)
  waiting for transfers between devices  80.2 us (15%)
  blocking collectives  73.7 us (14%)
  starting transfers between devices  71.6 us (13%)
  local copies, waits for them, and re-layouts  28.3 us (5%)
  other arithmetic  16.8 us (3%)
  between operations  15.4 us (3%)
    pallas_call x1, Pallas kernels, moe(): pl.pallas_call(functools.partial(expert_kernel, experts, cap), out_shape=...  157 us
    pallas_call x9, Pallas kernels, call(): pl.pallas_call(kernel, out_shape=[jax.ShapeDtypeStruct(s, d) for s, d in...  82.4 us
    psum x1, blocking collectives, shards(): small = lax.psum(small, ('expert', 'tensor'))  73.7 us
    ppermute x13, waiting for transfers between devices, swap(): return lax.ppermute(x, 'tensor', [(i, i ^ bit) for i in range(4)])  73.7 us
    all_to_all x2, starting transfers between devices, exchange(): lax.all_to_all(x.reshape(experts, cap, x.shape[-1]), 'expert', split_axis...  64.9 us
  transfers between devices with their start and end apart: 16, of which 6 were waited for; matrix products, arithmetic and copies ran while one was open for 7% of the time, Pallas kernels for 14%

commit v1 on v0

--- a/solution.py
+++ b/solution.py
@@ -68,32 +68,29 @@
 SM = pl.BlockSpec(memory_space=pltpu.SMEM)
 
 
-def route_kernel(experts, cap, nv_ref, routes_ref, grad_ref, packed_ref, slots_ref):
-    rows = grad_ref.shape[0]
-    routes = routes_ref[...]
-    first, second = routes[0:1], routes[1:2]
-    valid = iota((1, rows), 1) < nv_ref[0]
+def slot_lines(experts, cap, valid_count, routes):
+    rows = routes.shape[1]
+    valid = iota((1, rows), 1) < valid_count
     ids = iota((experts, rows), 0)
-    hot0 = ((ids == first) & valid).astype(F32)
-    hot1 = ((ids == second) & valid).astype(F32)
+    hot0 = ((ids == routes[0:1]) & valid).astype(F32)
+    hot1 = ((ids == routes[1:2]) & valid).astype(F32)
     before = (iota((rows, rows), 0) < iota((rows, rows), 1)).astype(BF)
     rank = dot((hot0 + hot1).astype(BF), before)
     place = ids.astype(F32) * cap + rank
     bad = jnp.where(valid, 0.0, 1.0)
     slot0 = jnp.sum(hot0 * place, axis=0, keepdims=True) - bad
     slot1 = jnp.sum(hot1 * place, axis=0, keepdims=True) - bad
+    return slot0, slot1
+
+
+def route_kernel(experts, cap, nv_ref, routes_ref, grad_ref, packed_ref, slots_ref):
+    rows = grad_ref.shape[0]
+    slot0, slot1 = slot_lines(experts, cap, nv_ref[0], routes_ref[...])
     spots = iota((experts * cap, rows), 0)
     pick0 = spots == slot0.astype(jnp.int32)
     pick1 = spots == slot1.astype(jnp.int32)
     packed_ref[...] = dot((pick0 | pick1).astype(BF), grad_ref[...]).astype(BF)
     slots_ref[...] = jnp.concatenate([slot0, slot1, jnp.zeros((6, rows), F32)], axis=0)
-
-
-def pick_matrix(slots_ref, spots):
-    rows = slots_ref.shape[1]
-    where = iota((spots, rows), 0)
-    slots = slots_ref[...].astype(jnp.int32)
-    return ((where == slots[0:1]) | (where == slots[1:2])).astype(BF)
 
 
 def back_matrix(slots_ref, spots):
@@ -282,42 +279,61 @@
         part_ref[...] = part
 
 
+def gates_of(experts, normed, router_t, routes):
+    rows = normed.shape[0]
+    logits = dot(router_t, normed, 1, 1)
+    ids = iota((experts, rows), 0)
+    signs = (ids == routes[0:1]).astype(F32) - (ids == routes[1:2]).astype(F32)
+    gap = jnp.sum(logits * signs, axis=0, keepdims=True)
+    return 1.0 / (1.0 + jnp.exp(-gap)), 1.0 / (1.0 + jnp.exp(gap))
+
+
+def meta_lines(gate, code):
+    rows = gate.shape[1]
+    line = iota((8, rows), 0)
+    high = gate.astype(BF).astype(F32)
+    mid = (gate - high).astype(BF).astype(F32)
+    low = gate - high - mid
+    picked = jnp.where(line == 0, high, jnp.where(line == 1, mid, jnp.where(line == 2, low, 0.0)))
+    return jnp.where(line == 3, code, picked).astype(BF)
+
+
+def hidden_rows(x_ref, keep_ref, got_ref, gain_ref, hidden_ref):
+    hidden = x_ref[...].astype(F32) + keep_ref[...] + got_ref[...].astype(F32)
+    hidden_ref[...] = hidden
+    return (hidden * rms(hidden) * gain_ref[...]).astype(BF)
+
+
 def middle_kernel(
     experts, cap, x_ref, keep_ref, got_ref, gain_ref, router_ref, routes_ref, slots_ref, hidden_ref, packed_ref, meta_ref
 ):
-    hidden = x_ref[...].astype(F32) + keep_ref[...] + got_ref[...].astype(F32)
-    hidden_ref[...] = hidden
-    normed = (hidden * rms(hidden) * gain_ref[...]).astype(BF)
-    rows = hidden.shape[0]
-    spots = experts * cap
+    normed = hidden_rows(x_ref, keep_ref, got_ref, gain_ref, hidden_ref)
     slots = slots_ref[...].astype(jnp.int32)
-    where = iota((spots, rows), 0)
+    routes = routes_ref[...]
+    where = iota((experts * cap, normed.shape[0]), 0)
     pick0 = where == slots[0:1]
     pick1 = where == slots[1:2]
     packed_ref[...] = dot((pick0 | pick1).astype(BF), normed).astype(BF)
-    logits = dot(router_ref[...], normed, 1, 1)
-    routes = routes_ref[...]
-    first, second = routes[0:1], routes[1:2]
-    ids = iota((experts, rows), 0)
-    gap = jnp.sum(
-        logits * ((ids == first).astype(F32) - (ids == second).astype(F32)), axis=0, keepdims=True
-    )
-    gate0 = 1.0 / (1.0 + jnp.exp(-gap))
-    gate1 = 1.0 / (1.0 + jnp.exp(gap))
-    line = iota((8, rows), 0)
-
-    def lines(gate, code):
-        high = gate.astype(BF).astype(F32)
-        mid = (gate - high).astype(BF).astype(F32)
-        low = gate - high - mid
-        picked = jnp.where(line == 0, high, jnp.where(line == 1, mid, jnp.where(line == 2, low, 0.0)))
-        return jnp.where(line == 3, (code + 1).astype(F32), picked).astype(BF)
-
-    meta = dot(lines(gate0, second), pick0.astype(BF), 1, 1) + dot(
-        lines(gate1, first), pick1.astype(BF), 1, 1
+    gate0, gate1 = gates_of(experts, normed, router_ref[...], routes)
+    codes = (routes + 1).astype(F32)
+    meta = dot(meta_lines(gate0, codes[1:2]), pick0.astype(BF), 1, 1) + dot(
+        meta_lines(gate1, codes[0:1]), pick1.astype(BF), 1, 1
     )
     for number in range(experts):
         meta_ref[number] = meta[:, number * cap : (number + 1) * cap]
+
+
+def middle_line_kernel(
+    experts, x_ref, keep_ref, got_ref, gain_ref, router_ref, routes_ref, slots_ref, hidden_ref, normed_ref, info_ref
+):
+    normed = hidden_rows(x_ref, keep_ref, got_ref, gain_ref, hidden_ref)
+    normed_ref[...] = normed
+    routes = routes_ref[...]
+    gate0, gate1 = gates_of(experts, normed, router_ref[...], routes)
+    codes = (routes + 1).astype(F32)
+    info_ref[...] = jnp.concatenate(
+        [slots_ref[0:2], gate0, gate1, codes, jnp.zeros((2, normed.shape[0]), F32)], axis=0
+    )
 
 
 def gelu_pair(v):
@@ -326,6 +342,64 @@
     t = jnp.tanh(v * (GELU + GELU * CUBIC * squared))
     half = 0.5 + 0.5 * t
     return v * half, half + 0.5 * v * (1.0 - t * t) * slope
+
+
+def flipped(me, k, count):
+    total, bit = 0, 1
+    while bit < count:
+        total = total + lax.rem(me // bit + k // bit, 2) * bit
+        bit *= 2
+    return total
+
+
+def weight_grads(chunks, span, xt_ref, geot_ref, act_ref, gi_ref, acc_ref, stage_ref, gw_ref, out_sem):
+    tiles = D // TILE
+
+    def store(step, slot):
+        q = step // (2 * tiles)
+        place = lax.rem(step, 2 * tiles)
+        return pltpu.make_async_copy(
+            stage_ref.at[slot],
+            gw_ref.at[q, pl.ds(pl.multiple_of(place * TILE, TILE), TILE)],
+            out_sem.at[slot],
+        )
+
+    def weights(step, carry):
+        q = step // (2 * tiles)
+        place = lax.rem(step, 2 * tiles)
+        slot = lax.rem(step, 2)
+
+        @pl.when(step >= 2)
+        def _():
+            store(step - 2, slot).wait()
+
+        def reduce(left_ref, right_ref, tile):
+            acc_ref[...] = jnp.zeros_like(acc_ref)
+
+            def one(j, c):
+                lines = pl.ds(pl.multiple_of(tile * TILE, TILE), TILE)
+                there = pl.ds(pl.multiple_of(j * span, span), span)
+                acc_ref[...] += dot(left_ref[j, lines], right_ref[q, there])
+                return c
+
+            lax.fori_loop(0, chunks, one, 0)
+            stage_ref[slot] = acc_ref[...].astype(BF)
+
+        @pl.when(place < tiles)
+        def _():
+            reduce(xt_ref, gi_ref, place)
+
+        @pl.when(place >= tiles)
+        def _():
+            reduce(geot_ref, act_ref, place - tiles)
+
+        store(step, slot).start()
+        return carry
+
+    steps = 8 * tiles
+    lax.fori_loop(0, steps, weights, 0)
+    for step in (steps - 2, steps - 1):
+        store(step, step % 2).wait()
 
 
 def expert_kernel(
@@ -338,10 +412,9 @@
     barrier = pltpu.get_barrier_semaphore()
 
     def peer(k):
-        return lax.rem(me + k, count)
-
-    def source(k):
-        return lax.rem(me + count - k, count)
+        return flipped(me, k, count)
+
+    source = peer
 
     def greet(k, carry):
         pl.semaphore_signal(
@@ -390,7 +463,8 @@
         send_rows(k).start()
         return carry
 
-    lax.fori_loop(1, count, start_sends, 0)
+    lax.fori_loop(count // 2, count, start_sends, 0)
+    lax.fori_loop(1, count // 2, start_sends, 0)
     own_rows = pltpu.make_async_copy(packed_ref.at[rows_of(me)], x_ref.at[rows_of(0)], local_sem.at[0])
     own_rows.start()
     own_meta = pltpu.make_async_copy(send_meta_ref.at[me], meta_ref.at[0], local_sem.at[1])
@@ -479,53 +553,7 @@
 
     lax.fori_loop(0, count // group, results, 0)
 
-    tiles = D // TILE
-
-    def store(step, slot):
-        q = step // (2 * tiles)
-        place = lax.rem(step, 2 * tiles)
-        return pltpu.make_async_copy(
-            stage_ref.at[slot],
-            gw_ref.at[q, pl.ds(pl.multiple_of(place * TILE, TILE), TILE)],
-            out_sem.at[slot],
-        )
-
-    def weights(step, carry):
-        q = step // (2 * tiles)
-        place = lax.rem(step, 2 * tiles)
-        slot = lax.rem(step, 2)
-
-        @pl.when(step >= 2)
-        def _():
-            store(step - 2, slot).wait()
-
-        def reduce(left_ref, right_ref, tile):
-            acc_ref[...] = jnp.zeros_like(acc_ref)
-
-            def one(j, c):
-                lines = pl.ds(pl.multiple_of(tile * TILE, TILE), TILE)
-                there = pl.ds(pl.multiple_of(j * span, span), span)
-                acc_ref[...] += dot(left_ref[j, lines], right_ref[q, there])
-                return c
-
-            lax.fori_loop(0, count // group, one, 0)
-            stage_ref[slot] = acc_ref[...].astype(BF)
-
-        @pl.when(place < tiles)
-        def _():
-            reduce(xt_ref, gi_ref, place)
-
-        @pl.when(place >= tiles)
-        def _():
-            reduce(geot_ref, act_ref, place - tiles)
-
-        store(step, slot).start()
-        return carry
-
-    steps = 8 * tiles
-    lax.fori_loop(0, steps, weights, 0)
-    for step in (steps - 2, steps - 1):
-        store(step, step % 2).wait()
+    weight_grads(count // group, span, xt_ref, geot_ref, act_ref, gi_ref, acc_ref, stage_ref, gw_ref, out_sem)
     own_back.wait()
 
     def finish(k, carry):
@@ -535,6 +563,256 @@
         return carry
 
     lax.fori_loop(1, count, finish, 0)
+
+
+def mesh_copy(src, dst, send_sem, recv_sem, target):
+    return pltpu.make_async_remote_copy(
+        src_ref=src,
+        dst_ref=dst,
+        send_sem=send_sem,
+        recv_sem=recv_sem,
+        device_id={"expert": target},
+        device_id_type=pl.DeviceIdType.MESH,
+    )
+
+
+LINE = 4
+
+
+def expert_line_kernel(
+    cap, normed_ref, info_in, grads_ref, router_ref, w0, w1, w2, w3,
+    came_ref, result_ref, gw_ref, grouter_ref,
+    w_ref, block_ref, info_ref, x_ref, xs_ref, meta_ref, ms_ref, xt_ref, geot_ref, act_ref, gi_ref, acc_ref, stage_ref,
+    b_send, b_recv, i_send, i_recv, x_send, x_recv, m_send, m_recv, r_send, r_recv, local_sem, w_sem, out_sem,
+):
+    count = 2 * LINE
+    me = lax.axis_index("expert")
+    place = me // 2
+    side = me - 2 * place
+    mate = me + 1 - 2 * side
+    barrier = pltpu.get_barrier_semaphore()
+
+    def greet(k, carry):
+        pl.semaphore_signal(
+            barrier,
+            inc=1,
+            device_id={"expert": lax.rem(me + k, count)},
+            device_id_type=pl.DeviceIdType.MESH,
+        )
+        return carry
+
+    lax.fori_loop(1, count, greet, 0)
+    pl.semaphore_wait(barrier, count - 1)
+
+    def along(block, step):
+        return (
+            mesh_copy(
+                info_ref.at[block],
+                info_ref.at[block],
+                i_send.at[(step + 1) // 2, block],
+                i_recv.at[block],
+                me + 2 * step,
+            ),
+            mesh_copy(
+                block_ref.at[block],
+                block_ref.at[block],
+                b_send.at[(step + 1) // 2, block],
+                b_recv.at[block],
+                me + 2 * step,
+            ),
+        )
+
+    def across(block):
+        return (
+            mesh_copy(ms_ref.at[block], meta_ref.at[1, block], m_send.at[block], m_recv.at[block], mate),
+            mesh_copy(xs_ref.at[block], x_ref.at[1, block], x_send.at[block], x_recv.at[block], mate),
+        )
+
+    def rows_of(number):
+        return pl.ds(pl.multiple_of(number * cap, cap), cap)
+
+    def origin(part, block):
+        return 2 * block + side + part * (1 - 2 * side)
+
+    def give_back(part, block):
+        return mesh_copy(
+            x_ref.at[part, block],
+            came_ref.at[rows_of(me)],
+            r_send.at[part, block],
+            r_recv.at[me],
+            origin(part, block),
+        )
+
+    def each(pair, act):
+        for one in pair:
+            act(one)
+
+    own = (
+        pltpu.make_async_copy(info_in, info_ref.at[place], local_sem.at[0]),
+        pltpu.make_async_copy(normed_ref, block_ref.at[place], local_sem.at[1]),
+    )
+    each(own, lambda c: c.start())
+    loads = [
+        pltpu.make_async_copy(w, w_ref.at[i], w_sem.at[i]) for i, w in enumerate((w0, w1, w2, w3))
+    ]
+    each(loads, lambda c: c.start())
+    each(own, lambda c: c.wait())
+
+    @pl.when(place < LINE - 1)
+    def _():
+        each(along(place, 1), lambda c: c.start())
+
+    @pl.when(place > 0)
+    def _():
+        each(along(place, -1), lambda c: c.start())
+
+    experts = router_ref.shape[1]
+    rows = normed_ref.shape[0]
+
+    def select(block):
+        info = info_ref[block]
+        slots = info[0:2].astype(jnp.int32)
+        lines0 = meta_lines(info[2:3], info[5:6])
+        lines1 = meta_lines(info[3:4], info[4:5])
+        for part, expert in ((1, mate), (0, me)):
+            where = iota((cap, rows), 0) + expert * cap
+            pick0 = where == slots[0:1]
+            pick1 = where == slots[1:2]
+            taken = dot((pick0 | pick1).astype(BF), block_ref[block]).astype(BF)
+            meta = dot(lines0, pick0.astype(BF), 1, 1) + dot(lines1, pick1.astype(BF), 1, 1)
+            if part:
+                xs_ref[block] = taken
+                ms_ref[block] = meta
+                each(across(block), lambda c: c.start())
+            else:
+                x_ref[0, block] = taken
+                meta_ref[0, block] = meta
+
+    select(place)
+    grouter_ref[...] = jnp.zeros_like(grouter_ref)
+    each(loads, lambda c: c.wait())
+    mirror = place // 2
+    inward = place + mirror * (LINE - 1 - 2 * place)
+
+    def block_at(i):
+        step = i + inward * (1 - i // 2 - 2 * (i // 2 - i // (LINE - 1)))
+        return step + mirror * (LINE - 1 - 2 * step)
+
+    def accept(distance):
+        for step in (-1, 1):
+            block = place + step * distance
+            inside = (block >= 0) & (block < LINE)
+
+            @pl.when(inside)
+            def _():
+                each(along(block, -step), lambda c: c.wait_recv())
+                ahead = place - step
+
+                @pl.when((ahead >= 0) & (ahead < LINE))
+                def _():
+                    each(along(block, -step), lambda c: c.start())
+
+        for step in (-1, 1):
+            block = place + step * distance
+            inside = (block >= 0) & (block < LINE)
+
+            @pl.when(inside)
+            def _():
+                select(block)
+
+    def chunk(c, carry):
+        for distance in range(1, LINE):
+
+            @pl.when(c == 2 * distance - 1)
+            def _():
+                accept(distance)
+
+        part = lax.rem(c + 1, 2) - (7 - c) // 7 + c // 7
+        block = block_at((c + 1) // 2 - part * ((c + 1) // 2 - (c - 1) // 2))
+
+        @pl.when(part == 1)
+        def _():
+            each(across(block), lambda c: c.wait_recv())
+
+        here = pl.ds(pl.multiple_of(c * cap, cap), cap)
+        meta = meta_ref[part, block].T
+        gate = meta[:, 0:1] + meta[:, 1:2] + meta[:, 2:3]
+        code = meta[:, 3:4].astype(jnp.int32)
+        geo = (gate * grads_ref[rows_of(origin(part, block)), :].astype(F32)).astype(BF)
+        x = x_ref[part, block]
+        xt_ref[c] = x.T
+        geot_ref[c] = geo.T
+        acc_ref[...] = jnp.zeros_like(acc_ref)
+
+        def quarter(q, worth):
+            inner = dot(x, w_ref[q, :D])
+            grad_active = dot(geo, w_ref[q, D:], 1, 1)
+            act, slope = gelu_pair(inner)
+            gi = (slope * grad_active).astype(BF)
+            act_ref[q, here] = act.astype(BF)
+            gi_ref[q, here] = gi
+            acc_ref[...] += dot(gi, w_ref[q, :D], 1, 1)
+            return worth + jnp.sum(act * grad_active, axis=1, keepdims=True)
+
+        worth = lax.fori_loop(0, 4, quarter, jnp.zeros((cap, 1), F32))
+        ids = iota((cap, experts), 1)
+        signs = (ids == me).astype(F32) - (ids + 1 == code).astype(F32)
+        share = jnp.where(code > 0, (1.0 - gate) * worth, 0.0) * signs
+        high = share.astype(BF)
+        low = (share - high.astype(F32)).astype(BF)
+        grouter_ref[...] += dot(high.T, x) + dot(low.T, x)
+        x_ref[part, block] = (acc_ref[...] + dot(high, router_ref[...], 1, 1)).astype(BF)
+
+        @pl.when(origin(part, block) != me)
+        def _():
+            give_back(part, block).start()
+
+        return carry
+
+    lax.fori_loop(0, count, chunk, 0)
+    own_back = pltpu.make_async_copy(x_ref.at[0, place], came_ref.at[rows_of(me)], local_sem.at[0])
+    own_back.start()
+
+    def results(c, carry):
+        part = lax.rem(c + 1, 2) - (7 - c) // 7 + c // 7
+        block = block_at((c + 1) // 2 - part * ((c + 1) // 2 - (c - 1) // 2))
+        here = pl.ds(pl.multiple_of(c * cap, cap), cap)
+        meta = meta_ref[part, block].T
+        gate = meta[:, 0:1] + meta[:, 1:2] + meta[:, 2:3]
+        acc_ref[...] = jnp.zeros_like(acc_ref)
+
+        def quarter(q, carry):
+            acc_ref[...] += dot(act_ref[q, here], w_ref[q, D:])
+            return carry
+
+        lax.fori_loop(0, 4, quarter, 0)
+        result_ref[rows_of(origin(part, block)), :] = (gate * acc_ref[...]).astype(BF)
+        return carry
+
+    lax.fori_loop(0, count, results, 0)
+    weight_grads(count, cap, xt_ref, geot_ref, act_ref, gi_ref, acc_ref, stage_ref, gw_ref, out_sem)
+    own_back.wait()
+
+    for block in range(LINE):
+        each(across(block), lambda c: c.wait_send())
+        for step in (-1, 1):
+            @pl.when((place + step >= 0) & (place + step < LINE) & ((place - block) * step >= 0))
+            def _():
+                each(along(block, step), lambda c: c.wait_send())
+
+        for part in (0, 1):
+
+            @pl.when(origin(part, block) != me)
+            def _():
+                give_back(part, block).wait_send()
+
+    for number in range(count):
+
+        @pl.when(number != me)
+        def _():
+            mesh_copy(
+                x_ref.at[0, 0], came_ref.at[rows_of(number)], r_send.at[0, 0], r_recv.at[number], mate
+            ).wait_recv()
 
 
 def turn_kernel(nv_ref, came_ref, slots_ref, hidden_ref, gain_ref, grad_ref, gh_ref, ga_ref, gain_out):
@@ -613,6 +891,57 @@
     )(packed, meta, grads, router, *quarters)
 
 
+def moe_line(experts, cap, normed, info, grads, router, quarters):
+    rows = normed.shape[0]
+    spots = experts * cap
+    anyspec = pl.BlockSpec(memory_space=pl.ANY)
+    dma = pltpu.SemaphoreType.DMA
+    return pl.pallas_call(
+        functools.partial(expert_line_kernel, cap),
+        out_shape=[
+            jax.ShapeDtypeStruct((spots, D), BF),
+            jax.ShapeDtypeStruct((spots, D), BF),
+            jax.ShapeDtypeStruct((4, 2 * D, D), BF),
+            jax.ShapeDtypeStruct((experts, D), F32),
+        ],
+        in_specs=[VM, VM, VM, VM] + [anyspec] * 4,
+        out_specs=[anyspec, VM, anyspec, VM],
+        scratch_shapes=[
+            pltpu.VMEM((4, 2 * D, D), BF),
+            pltpu.VMEM((LINE, rows, D), BF),
+            pltpu.VMEM((LINE, 8, rows), F32),
+            pltpu.VMEM((2, LINE, cap, D), BF),
+            pltpu.VMEM((LINE, cap, D), BF),
+            pltpu.VMEM((2, LINE, 8, cap), F32),
+            pltpu.VMEM((LINE, 8, cap), F32),
+            pltpu.VMEM((experts, D, cap), BF),
+            pltpu.VMEM((experts, D, cap), BF),
+            pltpu.VMEM((4, spots, D), BF),
+            pltpu.VMEM((4, spots, D), BF),
+            pltpu.VMEM((cap, D), F32),
+            pltpu.VMEM((2, TILE, D), BF),
+            dma((2, LINE)),
+            dma((LINE,)),
+            dma((2, LINE)),
+            dma((LINE,)),
+            dma((LINE,)),
+            dma((LINE,)),
+            dma((LINE,)),
+            dma((LINE,)),
+            dma((2, LINE)),
+            dma((experts,)),
+            dma((2,)),
+            dma((4,)),
+            dma((2,)),
+        ],
+        compiler_params=pltpu.CompilerParams(
+            collective_id=2, has_side_effects=True, vmem_limit_bytes=62 * MIB
+        ),
+        cost_estimate=pl.CostEstimate(flops=12 * spots * D * 4 * D, bytes_accessed=60 * MIB, transcendentals=0),
+        name="experts_line",
+    )(normed, info, grads, router, *quarters)
+
+
 def shards(
     inputs,
     lengths,
@@ -667,11 +996,11 @@
         ).reshape(x.shape)
 
     grads_in = exchange(packed_grad)
-    mine = jnp.concatenate([up_weight[0], down_weight[0]], axis=0)
+    mine, pair_w = lax.optimization_barrier(
+        (jnp.concatenate([up_weight[0], down_weight[0]], axis=0), pair_w)
+    )
     far = swap(mine, 2)
     side = swap(mine, 1)
-    cross = swap(far, 1)
-    quarters = [mine, side, far, cross]
 
     attn_cost = dict(
         flops=2 * SEQ * D * 4 * inner + heads * SEQ * SEQ * 160, moved=6 * MIB, exps=heads * SEQ * SEQ
@@ -695,20 +1024,35 @@
         **attn_cost,
     )
     got = swap(send, 1)
-    hidden, packed_rows, meta = call(
-        functools.partial(middle_kernel, experts, cap),
-        [((rows, D), F32), ((spots, D), BF), ((experts, 8, cap), F32)],
-        (inputs, keep, got, gain2, jnp.transpose(router_weight), routes_t, slots),
-        flops=2 * spots * rows * D,
-        moved=8 * MIB,
-        name="middle",
-    )
-    came, result, weight_grads, grad_router = moe(
-        experts, cap, packed_rows, meta, grads_in, router_weight, quarters
-    )
+    far, got = lax.optimization_barrier((far, got))
+    quarters = [mine, side, far, swap(far, 1)]
+    middle_args = (inputs, keep, got, gain2, jnp.transpose(router_weight), routes_t, slots)
+    if experts == 2 * LINE and cap == TILE:
+        hidden, normed_two, info = call(
+            functools.partial(middle_line_kernel, experts),
+            [((rows, D), F32), ((rows, D), BF), ((8, rows), F32)],
+            middle_args,
+            moved=6 * MIB,
+            name="middle",
+        )
+        came, result, weight_parts, grad_router = moe_line(
+            experts, cap, normed_two, info, grads_in, router_weight, quarters
+        )
+    else:
+        hidden, packed_rows, meta = call(
+            functools.partial(middle_kernel, experts, cap),
+            [((rows, D), F32), ((spots, D), BF), ((experts, 8, cap), F32)],
+            middle_args,
+            flops=2 * spots * rows * D,
+            moved=8 * MIB,
+            name="middle",
+        )
+        came, result, weight_parts, grad_router = moe(
+            experts, cap, packed_rows, meta, grads_in, router_weight, quarters
+        )
     came_out = exchange(result)
 
-    grads = weight_grads
+    grads = weight_parts
     near = grads[0].astype(F32) + swap(grads[1], 1).astype(F32)
     away = grads[2].astype(F32) + swap(grads[3], 1).astype(F32)
     grad_weights = near + swap(away.astype(BF), 2).astype(F32)

time: 536 us -> 456 us (0.85)
  the two profiles are of different devices: /device:TPU:0 before, /device:TPU:8 now
where the time goes in v1:
time: 456 us; the launch traced here: 451 us
  Pallas kernels  238 us (52%)
  blocking collectives  72.3 us (16%)
  waiting for transfers between devices  63.9 us (14%)
  local copies, waits for them, and re-layouts  24.8 us (5%)
  starting transfers between devices  20.1 us (4%)
  other arithmetic  17 us (4%)
  between operations  15.2 us (3%)
    pallas_call x1, Pallas kernels, moe_line(): pl.pallas_call(functools.partial(expert_line_kernel, cap), out_shape=[jax...  159 us
    pallas_call x9, Pallas kernels, call(): pl.pallas_call(kernel, out_shape=[jax.ShapeDtypeStruct(s, d) for s, d in...  78.8 us
    psum x1, blocking collectives, shards(): small = lax.psum(small, ('expert', 'tensor'))  72.3 us
    ppermute x13, waiting for transfers between devices, swap(): return lax.ppermute(x, 'tensor', [(i, i ^ bit) for i in range(4)])  56.6 us
    all_to_all x2, starting transfers between devices, exchange(): lax.all_to_all(x.reshape(experts, cap, x.shape[-1]), 'expert', split_axis...  12.9 us
  transfers between devices with their start and end apart: 16, of which 6 were waited for; matrix products, arithmetic and copies ran while one was open for 7% of the time, Pallas kernels for 16%

profile of v1, /device:TPU:8, one launch (start us, length us, event | category | flops | bytes accessed | tf_op | source)
XLA Modules:
  0.0 450.7 jit_solution(11887916520471022876)
XLA Ops:
  11.4 4.8 %route.1 = (bf16[2048,768]{1,0:T(8,128)(2,1)}, f32[8,512]{1,0:T(8,128)}) custom-call(s32[1]{0:T(128)} %bitcast.1.nv_ref, s32[2,512]{1,0:T(2,128)} %bitcast.44, bf16[512,768]{1,0:T(8,128)(2,1)} %grad_ref.3), custom_call_target="tpu_custom_call" | custom-call | flops 1610612736 | bytes 4194304 | tf_op jit(solution)/shard_map/route/pallas_call | solution.py:55
  16.1 6.4 %all-to-all-start = ((bf16[8,256,768]{2,1,0:T(8,128)(2,1)}), bf16[8,256,768]{2,1,0:T(8,128)(2,1)}, u32[]{:S(2)}, u32[]{:S(2)}) async-start(bf16[8,256,768]{2,1,0:T(8,128)(2,1)} %bitcast.35), calls=%async_computation | async-start | bytes 6291456 | tf_op jit(solution)/shard_map/all_to_all | solution.py:994
  22.6 3.3 pad_maximum_fusion.w0
  25.8 10.5 %collective-permute-done.2 = bf16[768,768]{1,0:T(8,128)(2,1)S(1)} collective-permute-done((bf16[768,768]{1,0:T(8,128)(2,1)S(1)}, bf16[768,768]{1,0:T(8,128)(2,1)S(1)}, u32[]{:S(2)}, u32[]{:S(2)}) %collective-permute-start.2) | collective-permute-done | bytes 1179680 | tf_op jit(solution)/shard_map/ppermute | solution.py:973
  41.2 10.0 %attend_own.1 = (bf16[1024,768]{1,0:T(8,128)(2,1)}, bf16[576,1024]{1,0:T(8,128)(2,1)}, bf16[192,1024]{1,0:T(8,128)(2,1)}, f32[8,1024]{1,0:T(8,128)}, f32[1024,768]{1,0:T(8,128)}) custom-call(s32[2]{0:T(128)} %pad_add_fusion.scal_ref, f32[32,3]{1,0:T(8,128)} %copy-done.6, bf16[512,768]{1,0:T(8,128)(2,1)} %x_ref.3, bf16[512,768]{1,0:T(8,128)(2,1)} %copy-done.13, ...), custom_call_target="tpu_custom_call" | custom-call | flops 1711276032 | bytes 6291456 | tf_op jit(solution)/shard_map/attend_own/pallas_call | solution.py:55
  52.9 36.2 %collective-permute-done.table_ref = f32[32,3]{1,0:T(8,128)S(1)} collective-permute-done((f32[32,3]{1,0:T(8,128)S(1)}, f32[32,3]{1,0:T(8,128)S(1)}, u32[]{:S(2)}, u32[]{:S(2)}) %collective-permute-start) | collective-permute-done | bytes 416 | tf_op jit(solution)/shard_map/ppermute | solution.py:973
  89.7 10.1 %attend_pair.1 = (bf16[576,1024]{1,0:T(8,128)(2,1)}, bf16[192,1024]{1,0:T(8,128)(2,1)}, f32[8,1024]{1,0:T(8,128)}, f32[512,768]{1,0:T(8,128)}, bf16[512,768]{1,0:T(8,128)(2,1)}) custom-call(s32[2]{0:T(128)} %pad_add_fusion.scal_ref, f32[32,3]{1,0:T(8,128)} %copy-done.14, bf16[1024,768]{1,0:T(8,128)(2,1)} %get-tuple-element.47.refs_0_, ...), custom_call_target="tpu_custom_call" | custom-call | flops 1711276032 | bytes 6291456 | tf_op jit(solution)/shard_map/attend_pair/pallas_call | solution.py:55
  100.3 3.1 collective-permute-done.4.got_ref
  105.0 3.6 middle.1
  109.2 158.8 %experts_line.1 = (bf16[2048,768]{1,0:T(8,128)(2,1)}, bf16[2048,768]{1,0:T(8,128)(2,1)}, bf16[4,1536,768]{2,1,0:T(8,128)(2,1)}, f32[8,768]{1,0:T(8,128)}) custom-call(bf16[512,768]{1,0:T(8,128)(2,1)} %get-tuple-element.55.normed_ref, f32[8,512]{1,0:T(8,128)} %get-tuple-element.56.info_in, bf16[2048,768]{1,0:T(8,128)(2,1)} %bitcast.11.grads_ref, ...), custom_call_target="tpu_custom_call" | custom-call | flops 57982058496 | bytes 62914560 | tf_op jit(solution)/shard_map/experts_line/pallas_call | solution.py:899
  268.0 4.1 slice_bitcast_fusion.3
  272.0 6.8 %turn.1 = (f32[512,768]{1,0:T(8,128)}, bf16[512,768]{1,0:T(8,128)(2,1)}, f32[8,768]{1,0:T(8,128)}) custom-call(s32[1]{0:T(128)} %bitcast.1.nv_ref, bf16[2048,768]{1,0:T(8,128)(2,1)} %get-tuple-element.64.came_ref, f32[8,512]{1,0:T(8,128)} %get-tuple-element.54.slots_ref, f32[512,768]{1,0:T(8,128)} %get-tuple-element.60.hidden_ref, ...), custom_call_target="tpu_custom_call" | custom-call | flops 1610612736 | bytes 8388608 | tf_op jit(solution)/shard_map/turn/pallas_call | solution.py:55
  279.4 6.5 %all-to-all-start.1 = ((bf16[8,256,768]{2,1,0:T(8,128)(2,1)}), bf16[8,256,768]{2,1,0:T(8,128)(2,1)}, u32[]{:S(2)}, u32[]{:S(2)}) async-start(bf16[8,256,768]{2,1,0:T(8,128)(2,1)} %bitcast.12), calls=%async_computation.1 | async-start | bytes 6291456 | tf_op jit(solution)/shard_map/all_to_all | solution.py:994
  287.0 16.3 %attend_pair_back.1 = (bf16[576,768]{1,0:T(8,128)(2,1)}, bf16[192,768]{1,0:T(8,128)(2,1)}, f32[8,128]{1,0:T(8,128)}, f32[1024,768]{1,0:T(8,128)}) custom-call(s32[2]{0:T(128)} %pad_add_fusion.scal_ref, f32[32,3]{1,0:T(8,128)} %copy-done.14, bf16[1024,768]{1,0:T(8,128)(2,1)} %get-tuple-element.47.refs_0_, bf16[576,768]{1,0:T(8,128)(2,1)} %slice.70.refs_1_, ...), custom_call_target="tpu_custom_call" | custom-call | flops 4278190080 | bytes 9437184 | tf_op jit(solution)/shard_map/attend_pair_back/pallas_call | solution.py:55
  306.3 3.0 fusion
  309.8 17.4 %attend_own_back.1 = (f32[576,768]{1,0:T(8,128)}, f32[192,768]{1,0:T(8,128)}, f32[8,128]{1,0:T(8,128)}, f32[512,768]{1,0:T(8,128)}, bf16[512,768]{1,0:T(8,128)(2,1)}) custom-call(s32[2]{0:T(128)} %pad_add_fusion.scal_ref, f32[32,3]{1,0:T(8,128)} %copy-done.6, bf16[1024,768]{1,0:T(8,128)(2,1)} %get-tuple-element.47.refs_0_, bf16[576,768]{1,0:T(8,128)(2,1)} %bitcast.41, ...), custom_call_target="tpu_custom_call" | custom-call | flops 4278190080 | bytes 9437184 | tf_op jit(solution)/shard_map/attend_own_back/pallas_call | solution.py:55
  327.2 6.3 %collective-permute-done.9 = bf16[768,768]{1,0:T(8,128)(2,1)S(1)} collective-permute-done((bf16[768,768]{1,0:T(8,128)(2,1)S(1)}, bf16[768,768]{1,0:T(8,128)(2,1)S(1)}, u32[]{:S(2)}, u32[]{:S(2)}) %collective-permute-start.9) | collective-permute-done | bytes 1179680 | tf_op jit(solution)/shard_map/ppermute | solution.py:973
  333.5 2.9 fusion.2
  340.2 4.1 last.1
  345.1 72.3 %psum.14 = f32[8064]{0:T(1024)S(1)} all-reduce(f32[8064]{0:T(1024)S(1)} %pad_maximum_fusion.3), channel_id=1, replica_groups=mesh['expert'=8,'tensor'=4] {'expert','tensor'}, use_global_device_ids=true, to_apply=%region_0.1 | all-reduce | flops 8064 | bytes 64512 | tf_op jit(solution)/shard_map/psum | solution.py:1126
  419.7 7.3 %all-reduce.2.cloned.1.call-done = bf16[768,768]{1,0:T(8,128)(2,1)} async-done(((bf16[768,768]{1,0:T(8,128)(2,1)}), bf16[768,768]{1,0:T(8,128)(2,1)}) %all-reduce.2.cloned.1.call-update) | async-done | bytes 1179664 | tf_op jit(solution)/shard_map/psum | solution.py:1108
  427.1 2.6 slice.89
  430.5 3.9 fusion.1
  438.0 5.6 %outputs.1 = bf16[512,768]{1,0:T(8,128)(2,1)} custom-call(s32[1]{0:T(128)} %bitcast.1.nv_ref, bf16[2048,768]{1,0:T(8,128)(2,1)} %bitcast.13.came_ref, f32[8,512]{1,0:T(8,128)} %get-tuple-element.54.slots_ref, f32[512,768]{1,0:T(8,128)} %get-tuple-element.60.hidden_ref), custom_call_target="tpu_custom_call" | custom-call | flops 1610612736 | bytes 8388608 | tf_op jit(solution)/shard_map/outputs/pallas_call | solution.py:55
  (91 shorter events, 29.8 us)
Async XLA Ops:
  8.5 27.8 %collective-permute-start.2 = (bf16[768,768]{1,0:T(8,128)(2,1)S(1)}, bf16[768,768]{1,0:T(8,128)(2,1)S(1)}, u32[]{:S(2)}, u32[]{:S(2)}) collective-permute-start(bf16[768,768]{1,0:T(8,128)(2,1)S(1)} %pad_maximum_fusion.1), channel_id=1, source_target_pairs={{0,2},{1,3},{2,0},{3,1},{4,6},{5,7},{6,4},{7,5},{8,10},{9,11},{10,... | collective-permute-start | bytes 3538952 | tf_op jit(solution)/shard_map/ppermute | solution.py:973
  16.1 92.6 %all-to-all-start = ((bf16[8,256,768]{2,1,0:T(8,128)(2,1)}), bf16[8,256,768]{2,1,0:T(8,128)(2,1)}, u32[]{:S(2)}, u32[]{:S(2)}) async-start(bf16[8,256,768]{2,1,0:T(8,128)(2,1)} %bitcast.35), calls=%async_computation | async-start | bytes 6291456 | tf_op jit(solution)/shard_map/all_to_all | solution.py:994
  22.5 15.3 %copy-start.1 = (bf16[512,768]{1,0:T(8,128)(2,1)S(1)}, bf16[512,768]{1,0:T(8,128)(2,1)}, u32[]{:S(2)}) copy-start(bf16[512,768]{1,0:T(8,128)(2,1)} %x_ref.3) | copy-start | bytes 2359300
  22.5 15.3 %copy-start.9 = (f32[32,3]{0,1:T(4,128)S(1)}, f32[32,3]{0,1:T(4,128)}, u32[]{:S(2)}) copy-start(f32[32,3]{0,1:T(4,128)} %param.18) | copy-start | bytes 1156
  22.6 15.9 %copy-start.7 = (f32[768]{0:T(1024)S(1)}, f32[768]{0:T(1024)}, u32[]{:S(2)}) copy-start(f32[768]{0:T(1024)} %param.15) | copy-start | bytes 9220
  36.3 67.1 %collective-permute-start.3 = (bf16[1536,768]{1,0:T(8,128)(2,1)}, bf16[1536,768]{1,0:T(8,128)(2,1)}, u32[]{:S(2)}, u32[]{:S(2)}) collective-permute-start(bf16[1536,768]{1,0:T(8,128)(2,1)} %pad_maximum_fusion.w0), channel_id=1, source_target_pairs={{0,2},{1,3},{2,0},{3,1},{4,6},{5,7},{6,4},{7,5},{8,10},{9,11},{10,... | collective-permute-start | bytes 7077896 | tf_op jit(solution)/shard_map/ppermute | solution.py:973
  37.8 2.4 collective-permute-start.1
  37.9 51.2 %collective-permute-start = (f32[32,3]{1,0:T(8,128)S(1)}, f32[32,3]{1,0:T(8,128)S(1)}, u32[]{:S(2)}, u32[]{:S(2)}) collective-permute-start(f32[32,3]{1,0:T(8,128)S(1)} %copy.27.table_ref), channel_id=1, source_target_pairs={{0,2},{1,3},{2,0},{3,1},{4,6},{5,7},{6,4},{7,5},{8,10},{9,11},{10,... | collective-permute-start | bytes 1160 | tf_op jit(solution)/shard_map/ppermute | solution.py:973
  89.7 13.8 %copy-start.8 = (f32[768]{0:T(1024)S(1)}, f32[768]{0:T(1024)}, u32[]{:S(2)}) copy-start(f32[768]{0:T(1024)} %param.19) | copy-start | bytes 9220
  89.7 14.5 %copy-start.5 = (bf16[768,8]{0,1:T(8,128)(2,1)S(1)}, bf16[768,8]{0,1:T(8,128)(2,1)}, u32[]{:S(2)}) copy-start(bf16[768,8]{0,1:T(8,128)(2,1)} %param.20) | copy-start | bytes 36868
  99.8 3.6 collective-permute-start.4
  99.8 8.9 %collective-permute-start.5 = (bf16[1536,768]{1,0:T(8,128)(2,1)}, bf16[1536,768]{1,0:T(8,128)(2,1)}, u32[]{:S(2)}, u32[]{:S(2)}) collective-permute-start(bf16[1536,768]{1,0:T(8,128)(2,1)} %pad_maximum_fusion.w0), channel_id=1, source_target_pairs={{0,1},{1,0},{2,3},{3,2},{4,5},{5,4},{6,7},{7,6},{8,9},{9,8},{10,11... | collective-permute-start | bytes 7077896 | tf_op jit(solution)/shard_map/ppermute | solution.py:973
  103.4 5.8 %collective-permute-start.6 = (bf16[1536,768]{1,0:T(8,128)(2,1)}, bf16[1536,768]{1,0:T(8,128)(2,1)}, u32[]{:S(2)}, u32[]{:S(2)}) collective-permute-start(bf16[1536,768]{1,0:T(8,128)(2,1)} %collective-permute-done.3.w2), channel_id=1, source_target_pairs={{0,1},{1,0},{2,3},{3,2},{4,5},{5,4},{6,7},{7,6},{8,9},{9,8},{10,11... | collective-permute-start | bytes 7077896 | tf_op jit(solution)/shard_map/ppermute | solution.py:973
  272.0 34.2 %collective-permute-start.11 = (bf16[1536,768]{1,0:T(8,128)(2,1)S(1)}, bf16[1536,768]{1,0:T(8,128)(2,1)}, u32[]{:S(2)}, u32[]{:S(2)}) collective-permute-start(bf16[1536,768]{1,0:T(8,128)(2,1)S(1)} %get-tuple-element.105), channel_id=1, source_target_pairs={{0,1},{1,0},{2,3},{3,2},{4,5},{5,4},{6,7},{7,6},{8,9},{9,8},{10,11... | collective-permute-start | bytes 7077896 | tf_op jit(solution)/shard_map/ppermute | solution.py:973
  278.9 7.3 %collective-permute-start.7 = (bf16[512,768]{1,0:T(8,128)(2,1)}, bf16[512,768]{1,0:T(8,128)(2,1)S(1)}, u32[]{:S(2)}, u32[]{:S(2)}) collective-permute-start(bf16[512,768]{1,0:T(8,128)(2,1)} %get-tuple-element.65.refs_6_), channel_id=1, source_target_pairs={{0,1},{1,0},{2,3},{3,2},{4,5},{5,4},{6,7},{7,6},{8,9},{9,8},{10,11... | collective-permute-start | bytes 2359304 | tf_op jit(solution)/shard_map/ppermute | solution.py:973
  279.4 158.7 %all-to-all-start.1 = ((bf16[8,256,768]{2,1,0:T(8,128)(2,1)}), bf16[8,256,768]{2,1,0:T(8,128)(2,1)}, u32[]{:S(2)}, u32[]{:S(2)}) async-start(bf16[8,256,768]{2,1,0:T(8,128)(2,1)} %bitcast.12), calls=%async_computation.1 | async-start | bytes 6291456 | tf_op jit(solution)/shard_map/all_to_all | solution.py:994
  285.9 141.2 %all-reduce.2.cloned.1.call-start = ((), (), s32[]{:S(2)}) async-start(), calls=%async_computation.2 | async-start | bytes 2359296 | tf_op jit(solution)/shard_map/psum | solution.py:1108
  286.0 144.5 %collective-permute-start.10 = (bf16[1536,768]{1,0:T(8,128)(2,1)}, bf16[1536,768]{1,0:T(8,128)(2,1)}, u32[]{:S(2)}, u32[]{:S(2)}) collective-permute-start(bf16[1536,768]{1,0:T(8,128)(2,1)} %get-tuple-element.104), channel_id=1, source_target_pairs={{0,1},{1,0},{2,3},{3,2},{4,5},{5,4},{6,7},{7,6},{8,9},{9,8},{10,11... | collective-permute-start | bytes 7077896 | tf_op jit(solution)/shard_map/ppermute | solution.py:973
  304.7 28.8 %collective-permute-start.9 = (bf16[768,768]{1,0:T(8,128)(2,1)S(1)}, bf16[768,768]{1,0:T(8,128)(2,1)S(1)}, u32[]{:S(2)}, u32[]{:S(2)}) collective-permute-start(bf16[768,768]{1,0:T(8,128)(2,1)S(1)} %pad_maximum_fusion.2), channel_id=1, source_target_pairs={{0,2},{1,3},{2,0},{3,1},{4,6},{5,7},{6,4},{7,5},{8,10},{9,11},{10,... | collective-permute-start | bytes 3538952 | tf_op jit(solution)/shard_map/ppermute | solution.py:973
  309.2 121.3 %collective-permute-start.12 = (bf16[1536,768]{1,0:T(8,128)(2,1)S(1)}, bf16[1536,768]{1,0:T(8,128)(2,1)}, u32[]{:S(2)}, u32[]{:S(2)}) collective-permute-start(bf16[1536,768]{1,0:T(8,128)(2,1)S(1)} %fusion), channel_id=1, source_target_pairs={{0,2},{1,3},{2,0},{3,1},{4,6},{5,7},{6,4},{7,5},{8,10},{9,11},{10,... | collective-permute-start | bytes 7077896 | tf_op jit(solution)/shard_map/ppermute | solution.py:973
  327.2 12.1 %collective-permute-start.8 = (bf16[512,768]{1,0:T(8,128)(2,1)}, bf16[512,768]{1,0:T(8,128)(2,1)S(1)}, u32[]{:S(2)}, u32[]{:S(2)}) collective-permute-start(bf16[512,768]{1,0:T(8,128)(2,1)} %get-tuple-element.71), channel_id=1, source_target_pairs={{0,1},{1,0},{2,3},{3,2},{4,5},{5,4},{6,7},{7,6},{8,9},{9,8},{10,11... | collective-permute-start | bytes 2359304 | tf_op jit(solution)/shard_map/ppermute | solution.py:973
  333.5 5.5 %copy-start.11 = (f32[8,128]{1,0:T(8,128)S(1)}, f32[8,128]{1,0:T(8,128)}, u32[]{:S(2)}) copy-start(f32[8,128]{1,0:T(8,128)} %get-tuple-element.77) | copy-start | bytes 12292
  333.5 5.6 %copy-start.10 = (f32[8,128]{1,0:T(8,128)S(1)}, f32[8,128]{1,0:T(8,128)}, u32[]{:S(2)}) copy-start(f32[8,128]{1,0:T(8,128)} %get-tuple-element.78) | copy-start | bytes 12292
  340.2 4.8 %copy-start.4 = (f32[6144]{0:T(1024)S(1)}, f32[6144]{0:T(1024)}, u32[]{:S(2)}) copy-start(f32[6144]{0:T(1024)} %reshape.111) | copy-start | bytes 73732
  (8 other events, 12.8 us)
Sparse Core Ops, SparseCore 0:
  336.6 90.3 all-reduce.1

commit v2 on v1

--- a/solution.py
+++ b/solution.py
@@ -352,54 +352,74 @@
     return total
 
 
-def weight_grads(chunks, span, xt_ref, geot_ref, act_ref, gi_ref, acc_ref, stage_ref, gw_ref, out_sem):
+def weight_grads(xt_ref, geot_ref, act_ref, gi_ref, stage_ref, gw_ref, out_sem):
     tiles = D // TILE
+    steps = 8 * tiles
+
+    def columns(step):
+        return pl.ds(pl.multiple_of(lax.rem(step, tiles) * TILE, TILE), TILE)
 
     def store(step, slot):
-        q = step // (2 * tiles)
-        place = lax.rem(step, 2 * tiles)
+        half = lax.rem(step, 2 * tiles) // tiles
         return pltpu.make_async_copy(
             stage_ref.at[slot],
-            gw_ref.at[q, pl.ds(pl.multiple_of(place * TILE, TILE), TILE)],
+            gw_ref.at[step // (2 * tiles), pl.ds(pl.multiple_of(half * D, D), D), columns(step)],
             out_sem.at[slot],
         )
 
     def weights(step, carry):
         q = step // (2 * tiles)
-        place = lax.rem(step, 2 * tiles)
+        half = lax.rem(step, 2 * tiles) // tiles
         slot = lax.rem(step, 2)
 
         @pl.when(step >= 2)
         def _():
             store(step - 2, slot).wait()
 
-        def reduce(left_ref, right_ref, tile):
-            acc_ref[...] = jnp.zeros_like(acc_ref)
-
-            def one(j, c):
-                lines = pl.ds(pl.multiple_of(tile * TILE, TILE), TILE)
-                there = pl.ds(pl.multiple_of(j * span, span), span)
-                acc_ref[...] += dot(left_ref[j, lines], right_ref[q, there])
-                return c
-
-            lax.fori_loop(0, chunks, one, 0)
-            stage_ref[slot] = acc_ref[...].astype(BF)
-
-        @pl.when(place < tiles)
+        @pl.when(half == 0)
         def _():
-            reduce(xt_ref, gi_ref, place)
-
-        @pl.when(place >= tiles)
+            stage_ref[slot] = dot(xt_ref[...], gi_ref[q, :, columns(step)]).astype(BF)
+
+        @pl.when(half == 1)
         def _():
-            reduce(geot_ref, act_ref, place - tiles)
+            stage_ref[slot] = dot(geot_ref[...], act_ref[q, :, columns(step)]).astype(BF)
 
         store(step, slot).start()
         return carry
 
-    steps = 8 * tiles
     lax.fori_loop(0, steps, weights, 0)
     for step in (steps - 2, steps - 1):
         store(step, step % 2).wait()
+
+
+def expert_rows(x, geo, here, w_ref, xt_ref, geot_ref, act_ref, gi_ref, acc_ref):
+    xt_ref[:, here] = x.T
+    geot_ref[:, here] = geo.T
+    worth = 0.0
+    for q in range(4):
+        inner = dot(x, w_ref[q, :D])
+        grad_active = dot(geo, w_ref[q, D:], 1, 1)
+        act, slope = gelu_pair(inner)
+        gi = (slope * grad_active).astype(BF)
+        act_ref[q, here] = act.astype(BF)
+        gi_ref[q, here] = gi
+        back = dot(gi, w_ref[q, :D], 1, 1)
+        if q == 0:
+            acc_ref[...] = back
+        else:
+            acc_ref[...] += back
+        worth = worth + jnp.sum(act * grad_active, axis=1, keepdims=True)
+    return worth
+
+
+def expert_outs(start, size, column, act_ref, w_ref):
+    here = pl.ds(pl.multiple_of(start, size), size)
+    cols = pl.ds(pl.multiple_of(column * TILE, TILE), TILE)
+    total = None
+    for q in range(4):
+        term = dot(act_ref[q, here], w_ref[q, D:, cols])
+        total = term if total is None else total + term
+    return cols, total
 
 
 def expert_kernel(
@@ -499,22 +519,7 @@
         gy = jnp.concatenate([grads_ref[rows_of(source(j * group + i)), :] for i in range(group)], axis=0)
         geo = (gate * gy.astype(F32)).astype(BF)
         x = x_ref[here, :]
-        xt = x.T
-        xt_ref[j] = xt
-        geot_ref[j] = geo.T
-        acc_ref[...] = jnp.zeros_like(acc_ref)
-
-        def quarter(q, worth):
-            inner = dot(x, w_ref[q, :D])
-            grad_active = dot(geo, w_ref[q, D:], 1, 1)
-            act, slope = gelu_pair(inner)
-            gi = (slope * grad_active).astype(BF)
-            act_ref[q, here] = act.astype(BF)
-            gi_ref[q, here] = gi
-            acc_ref[...] += dot(gi, w_ref[q, :D], 1, 1)
-            return worth + jnp.sum(act * grad_active, axis=1, keepdims=True)
-
-        worth = lax.fori_loop(0, 4, quarter, jnp.zeros((span, 1), F32))
+        worth = expert_rows(x, geo, here, w_ref, xt_ref, geot_ref, act_ref, gi_ref, acc_ref)
         ids = iota((span, experts), 1)
         signs = (ids == me).astype(F32) - (ids + 1 == code).astype(F32)
         share = jnp.where(code > 0, (1.0 - gate) * worth, 0.0) * signs
@@ -535,25 +540,18 @@
     own_back = pltpu.make_async_copy(gsend_ref.at[rows_of(0)], came_ref.at[rows_of(me)], local_sem.at[0])
     own_back.start()
 
-    def results(j, carry):
-        here = pl.ds(pl.multiple_of(j * span, span), span)
+    def results(step, carry):
+        j = step // (D // TILE)
         meta = jnp.concatenate([meta_ref[j * group + i].T for i in range(group)], axis=0)
         gate = meta[:, 0:1] + meta[:, 1:2] + meta[:, 2:3]
-        acc_ref[...] = jnp.zeros_like(acc_ref)
-
-        def quarter(q, c):
-            acc_ref[...] += dot(act_ref[q, here], w_ref[q, D:])
-            return c
-
-        lax.fori_loop(0, 4, quarter, 0)
-        out = (gate * acc_ref[...]).astype(BF)
+        cols, total = expert_outs(j * span, span, lax.rem(step, D // TILE), act_ref, w_ref)
+        out = (gate * total).astype(BF)
         for i in range(group):
-            result_ref[rows_of(source(j * group + i)), :] = out[i * cap : (i + 1) * cap]
+            result_ref[rows_of(source(j * group + i)), cols] = out[i * cap : (i + 1) * cap]
         return carry
 
-    lax.fori_loop(0, count // group, results, 0)
-
-    weight_grads(count // group, span, xt_ref, geot_ref, act_ref, gi_ref, acc_ref, stage_ref, gw_ref, out_sem)
+    lax.fori_loop(0, count // group * (D // TILE), results, 0)
+    weight_grads(xt_ref, geot_ref, act_ref, gi_ref, stage_ref, gw_ref, out_sem)
     own_back.wait()
 
     def finish(k, carry):
@@ -698,6 +696,10 @@
         step = i + inward * (1 - i // 2 - 2 * (i // 2 - i // (LINE - 1)))
         return step + mirror * (LINE - 1 - 2 * step)
 
+    def chunk_at(c):
+        part = lax.rem(c + 1, 2) - (7 - c) // 7 + c // 7
+        return part, block_at((c + 1) // 2 - part * ((c + 1) // 2 - (c - 1) // 2))
+
     def accept(distance):
         for step in (-1, 1):
             block = place + step * distance
@@ -727,8 +729,7 @@
             def _():
                 accept(distance)
 
-        part = lax.rem(c + 1, 2) - (7 - c) // 7 + c // 7
-        block = block_at((c + 1) // 2 - part * ((c + 1) // 2 - (c - 1) // 2))
+        part, block = chunk_at(c)
 
         @pl.when(part == 1)
         def _():
@@ -740,21 +741,7 @@
         code = meta[:, 3:4].astype(jnp.int32)
         geo = (gate * grads_ref[rows_of(origin(part, block)), :].astype(F32)).astype(BF)
         x = x_ref[part, block]
-        xt_ref[c] = x.T
-        geot_ref[c] = geo.T
-        acc_ref[...] = jnp.zeros_like(acc_ref)
-
-        def quarter(q, worth):
-            inner = dot(x, w_ref[q, :D])
-            grad_active = dot(geo, w_ref[q, D:], 1, 1)
-            act, slope = gelu_pair(inner)
-            gi = (slope * grad_active).astype(BF)
-            act_ref[q, here] = act.astype(BF)
-            gi_ref[q, here] = gi
-            acc_ref[...] += dot(gi, w_ref[q, :D], 1, 1)
-            return worth + jnp.sum(act * grad_active, axis=1, keepdims=True)
-
-        worth = lax.fori_loop(0, 4, quarter, jnp.zeros((cap, 1), F32))
+        worth = expert_rows(x, geo, here, w_ref, xt_ref, geot_ref, act_ref, gi_ref, acc_ref)
         ids = iota((cap, experts), 1)
         signs = (ids == me).astype(F32) - (ids + 1 == code).astype(F32)
         share = jnp.where(code > 0, (1.0 - gate) * worth, 0.0) * signs
@@ -773,24 +760,20 @@
     own_back = pltpu.make_async_copy(x_ref.at[0, place], came_ref.at[rows_of(me)], local_sem.at[0])
     own_back.start()
 
-    def results(c, carry):
-        part = lax.rem(c + 1, 2) - (7 - c) // 7 + c // 7
-        block = block_at((c + 1) // 2 - part * ((c + 1) // 2 - (c - 1) // 2))
-        here = pl.ds(pl.multiple_of(c * cap, cap), cap)
-        meta = meta_ref[part, block].T
-        gate = meta[:, 0:1] + meta[:, 1:2] + meta[:, 2:3]
-        acc_ref[...] = jnp.zeros_like(acc_ref)
-
-        def quarter(q, carry):
-            acc_ref[...] += dot(act_ref[q, here], w_ref[q, D:])
-            return carry
-
-        lax.fori_loop(0, 4, quarter, 0)
-        result_ref[rows_of(origin(part, block)), :] = (gate * acc_ref[...]).astype(BF)
+    def results(step, carry):
+        first = step // (D // TILE) * LINE
+        cols, total = expert_outs(first * cap, LINE * cap, lax.rem(step, D // TILE), act_ref, w_ref)
+        for i in range(LINE):
+            part, block = chunk_at(first + i)
+            meta = meta_ref[part, block].T
+            gate = meta[:, 0:1] + meta[:, 1:2] + meta[:, 2:3]
+            result_ref[rows_of(origin(part, block)), cols] = (
+                gate * total[i * cap : (i + 1) * cap]
+            ).astype(BF)
         return carry
 
-    lax.fori_loop(0, count, results, 0)
-    weight_grads(count, cap, xt_ref, geot_ref, act_ref, gi_ref, acc_ref, stage_ref, gw_ref, out_sem)
+    lax.fori_loop(0, 2 * (D // TILE), results, 0)
+    weight_grads(xt_ref, geot_ref, act_ref, gi_ref, stage_ref, gw_ref, out_sem)
     own_back.wait()
 
     for block in range(LINE):
@@ -849,7 +832,6 @@
 
 def moe(experts, cap, packed, meta, grads, router, quarters):
     spots = experts * cap
-    groups = spots // CHUNK
     anyspec = pl.BlockSpec(memory_space=pl.ANY)
     dma = pltpu.SemaphoreType.DMA
     return pl.pallas_call(
@@ -865,14 +847,14 @@
         scratch_shapes=[
             pltpu.VMEM((4, 2 * D, D), BF),
             pltpu.VMEM((spots, D), BF),
-            pltpu.VMEM((groups, D, CHUNK), BF),
-            pltpu.VMEM((groups, D, CHUNK), BF),
+            pltpu.VMEM((D, spots), BF),
+            pltpu.VMEM((D, spots), BF),
             pltpu.VMEM((4, spots, D), BF),
             pltpu.VMEM((4, spots, D), BF),
             pltpu.VMEM((spots, D), BF),
             pltpu.VMEM((experts, 8, cap), F32),
             pltpu.VMEM((CHUNK, D), F32),
-            pltpu.VMEM((2, CHUNK, D), BF),
+            pltpu.VMEM((2, D, TILE), BF),
             dma((experts,)),
             dma((experts,)),
             dma((experts,)),
@@ -914,12 +896,12 @@
             pltpu.VMEM((LINE, cap, D), BF),
             pltpu.VMEM((2, LINE, 8, cap), F32),
             pltpu.VMEM((LINE, 8, cap), F32),
-            pltpu.VMEM((experts, D, cap), BF),
-            pltpu.VMEM((experts, D, cap), BF),
+            pltpu.VMEM((D, spots), BF),
+            pltpu.VMEM((D, spots), BF),
             pltpu.VMEM((4, spots, D), BF),
             pltpu.VMEM((4, spots, D), BF),
             pltpu.VMEM((cap, D), F32),
-            pltpu.VMEM((2, TILE, D), BF),
+            pltpu.VMEM((2, D, TILE), BF),
             dma((2, LINE)),
             dma((LINE,)),
             dma((2, LINE)),

time: 456 us -> 415 us (0.910)
  Pallas kernels: 238 us -> 200 us
    pallas_call x1, Pallas kernels: 159 us -> 121 us  [moe_line(): pl.pallas_call(functools.partial(expert_line_kernel, cap), out_shape=[jax...]
  transfers between devices with their start and end apart: 16 -> 16, of which waited for: 6 -> 6; matrix products, arithmetic and copies ran while one was open for 7% -> 8% of each run, Pallas kernels for 16% -> 18%
where the time goes in v2:
time: 415 us; the launch traced here: 410 us
  Pallas kernels  200 us (48%)
  blocking collectives  72 us (17%)
  waiting for transfers between devices  63.8 us (15%)
  local copies, waits for them, and re-layouts  24.8 us (6%)
  starting transfers between devices  18 us (4%)
  other arithmetic  17 us (4%)
  between operations  15.2 us (4%)
    pallas_call x1, Pallas kernels, moe_line(): pl.pallas_call(functools.partial(expert_line_kernel, cap), out_shape=[jax...  121 us
    pallas_call x9, Pallas kernels, call(): pl.pallas_call(kernel, out_shape=[jax.ShapeDtypeStruct(s, d) for s, d in...  78.8 us
    psum x1, blocking collectives, shards(): small = lax.psum(small, ('expert', 'tensor'))  72 us
    ppermute x13, waiting for transfers between devices, swap(): return lax.ppermute(x, 'tensor', [(i, i ^ bit) for i in range(4)])  56.6 us
    all_to_all x2, starting transfers between devices, exchange(): lax.all_to_all(x.reshape(experts, cap, x.shape[-1]), 'expert', split_axis...  10.8 us
  transfers between devices with their start and end apart: 16, of which 6 were waited for; matrix products, arithmetic and copies ran while one was open for 8% of the time, Pallas kernels for 18%

profile of v2, /device:TPU:8, one launch (start us, length us, event | category | flops | bytes accessed | tf_op | source)
XLA Modules:
  0.0 410.4 jit_solution(12669902520274436015)
XLA Ops:
  11.4 4.8 %route.1 = (bf16[2048,768]{1,0:T(8,128)(2,1)}, f32[8,512]{1,0:T(8,128)}) custom-call(s32[1]{0:T(128)} %bitcast.1.nv_ref, s32[2,512]{1,0:T(2,128)} %bitcast.44, bf16[512,768]{1,0:T(8,128)(2,1)} %grad_ref.3), custom_call_target="tpu_custom_call" | custom-call | flops 1610612736 | bytes 4194304 | tf_op jit(solution)/shard_map/route/pallas_call | solution.py:55
  16.1 6.4 %all-to-all-start = ((bf16[8,256,768]{2,1,0:T(8,128)(2,1)}), bf16[8,256,768]{2,1,0:T(8,128)(2,1)}, u32[]{:S(2)}, u32[]{:S(2)}) async-start(bf16[8,256,768]{2,1,0:T(8,128)(2,1)} %bitcast.35), calls=%async_computation | async-start | bytes 6291456 | tf_op jit(solution)/shard_map/all_to_all | solution.py:976
  22.6 3.3 pad_maximum_fusion.w0
  25.8 10.5 %collective-permute-done.2 = bf16[768,768]{1,0:T(8,128)(2,1)S(1)} collective-permute-done((bf16[768,768]{1,0:T(8,128)(2,1)S(1)}, bf16[768,768]{1,0:T(8,128)(2,1)S(1)}, u32[]{:S(2)}, u32[]{:S(2)}) %collective-permute-start.2) | collective-permute-done | bytes 1179680 | tf_op jit(solution)/shard_map/ppermute | solution.py:955
  41.2 10.0 %attend_own.1 = (bf16[1024,768]{1,0:T(8,128)(2,1)}, bf16[576,1024]{1,0:T(8,128)(2,1)}, bf16[192,1024]{1,0:T(8,128)(2,1)}, f32[8,1024]{1,0:T(8,128)}, f32[1024,768]{1,0:T(8,128)}) custom-call(s32[2]{0:T(128)} %pad_add_fusion.scal_ref, f32[32,3]{1,0:T(8,128)} %copy-done.6, bf16[512,768]{1,0:T(8,128)(2,1)} %x_ref.3, bf16[512,768]{1,0:T(8,128)(2,1)} %copy-done.13, ...), custom_call_target="tpu_custom_call" | custom-call | flops 1711276032 | bytes 6291456 | tf_op jit(solution)/shard_map/attend_own/pallas_call | solution.py:55
  52.9 36.2 %collective-permute-done.table_ref = f32[32,3]{1,0:T(8,128)S(1)} collective-permute-done((f32[32,3]{1,0:T(8,128)S(1)}, f32[32,3]{1,0:T(8,128)S(1)}, u32[]{:S(2)}, u32[]{:S(2)}) %collective-permute-start) | collective-permute-done | bytes 416 | tf_op jit(solution)/shard_map/ppermute | solution.py:955
  89.7 10.1 %attend_pair.1 = (bf16[576,1024]{1,0:T(8,128)(2,1)}, bf16[192,1024]{1,0:T(8,128)(2,1)}, f32[8,1024]{1,0:T(8,128)}, f32[512,768]{1,0:T(8,128)}, bf16[512,768]{1,0:T(8,128)(2,1)}) custom-call(s32[2]{0:T(128)} %pad_add_fusion.scal_ref, f32[32,3]{1,0:T(8,128)} %copy-done.14, bf16[1024,768]{1,0:T(8,128)(2,1)} %get-tuple-element.47.refs_0_, ...), custom_call_target="tpu_custom_call" | custom-call | flops 1711276032 | bytes 6291456 | tf_op jit(solution)/shard_map/attend_pair/pallas_call | solution.py:55
  100.3 3.1 collective-permute-done.4.got_ref
  105.0 3.6 middle.1
  109.2 121.0 %experts_line.1 = (bf16[2048,768]{1,0:T(8,128)(2,1)}, bf16[2048,768]{1,0:T(8,128)(2,1)}, bf16[4,1536,768]{2,1,0:T(8,128)(2,1)}, f32[8,768]{1,0:T(8,128)}) custom-call(bf16[512,768]{1,0:T(8,128)(2,1)} %get-tuple-element.55.normed_ref, f32[8,512]{1,0:T(8,128)} %get-tuple-element.56.info_in, bf16[2048,768]{1,0:T(8,128)(2,1)} %bitcast.11.grads_ref, ...), custom_call_target="tpu_custom_call" | custom-call | flops 57982058496 | bytes 62914560 | tf_op jit(solution)/shard_map/experts_line/pallas_call | solution.py:881
  230.2 4.1 slice_bitcast_fusion.3
  234.3 6.8 %turn.1 = (f32[512,768]{1,0:T(8,128)}, bf16[512,768]{1,0:T(8,128)(2,1)}, f32[8,768]{1,0:T(8,128)}) custom-call(s32[1]{0:T(128)} %bitcast.1.nv_ref, bf16[2048,768]{1,0:T(8,128)(2,1)} %get-tuple-element.64.came_ref, f32[8,512]{1,0:T(8,128)} %get-tuple-element.54.slots_ref, f32[512,768]{1,0:T(8,128)} %get-tuple-element.60.hidden_ref, ...), custom_call_target="tpu_custom_call" | custom-call | flops 1610612736 | bytes 8388608 | tf_op jit(solution)/shard_map/turn/pallas_call | solution.py:55
  241.6 4.4 %all-to-all-start.1 = ((bf16[8,256,768]{2,1,0:T(8,128)(2,1)}), bf16[8,256,768]{2,1,0:T(8,128)(2,1)}, u32[]{:S(2)}, u32[]{:S(2)}) async-start(bf16[8,256,768]{2,1,0:T(8,128)(2,1)} %bitcast.12), calls=%async_computation.1 | async-start | bytes 6291456 | tf_op jit(solution)/shard_map/all_to_all | solution.py:976
  247.2 16.3 %attend_pair_back.1 = (bf16[576,768]{1,0:T(8,128)(2,1)}, bf16[192,768]{1,0:T(8,128)(2,1)}, f32[8,128]{1,0:T(8,128)}, f32[1024,768]{1,0:T(8,128)}) custom-call(s32[2]{0:T(128)} %pad_add_fusion.scal_ref, f32[32,3]{1,0:T(8,128)} %copy-done.14, bf16[1024,768]{1,0:T(8,128)(2,1)} %get-tuple-element.47.refs_0_, bf16[576,768]{1,0:T(8,128)(2,1)} %slice.70.refs_1_, ...), custom_call_target="tpu_custom_call" | custom-call | flops 4278190080 | bytes 9437184 | tf_op jit(solution)/shard_map/attend_pair_back/pallas_call | solution.py:55
  266.5 3.0 fusion
  270.0 17.4 %attend_own_back.1 = (f32[576,768]{1,0:T(8,128)}, f32[192,768]{1,0:T(8,128)}, f32[8,128]{1,0:T(8,128)}, f32[512,768]{1,0:T(8,128)}, bf16[512,768]{1,0:T(8,128)(2,1)}) custom-call(s32[2]{0:T(128)} %pad_add_fusion.scal_ref, f32[32,3]{1,0:T(8,128)} %copy-done.6, bf16[1024,768]{1,0:T(8,128)(2,1)} %get-tuple-element.47.refs_0_, bf16[576,768]{1,0:T(8,128)(2,1)} %bitcast.41, ...), custom_call_target="tpu_custom_call" | custom-call | flops 4278190080 | bytes 9437184 | tf_op jit(solution)/shard_map/attend_own_back/pallas_call | solution.py:55
  287.4 6.3 %collective-permute-done.9 = bf16[768,768]{1,0:T(8,128)(2,1)S(1)} collective-permute-done((bf16[768,768]{1,0:T(8,128)(2,1)S(1)}, bf16[768,768]{1,0:T(8,128)(2,1)S(1)}, u32[]{:S(2)}, u32[]{:S(2)}) %collective-permute-start.9) | collective-permute-done | bytes 1179680 | tf_op jit(solution)/shard_map/ppermute | solution.py:955
  293.7 2.9 fusion.2
  300.4 4.1 last.1
  305.3 72.0 %psum.14 = f32[8064]{0:T(1024)S(1)} all-reduce(f32[8064]{0:T(1024)S(1)} %pad_maximum_fusion.3), channel_id=1, replica_groups=mesh['expert'=8,'tensor'=4] {'expert','tensor'}, use_global_device_ids=true, to_apply=%region_0.1 | all-reduce | flops 8064 | bytes 64512 | tf_op jit(solution)/shard_map/psum | solution.py:1108
  379.6 7.2 %all-reduce.2.cloned.1.call-done = bf16[768,768]{1,0:T(8,128)(2,1)} async-done(((bf16[768,768]{1,0:T(8,128)(2,1)}), bf16[768,768]{1,0:T(8,128)(2,1)}) %all-reduce.2.cloned.1.call-update) | async-done | bytes 1179664 | tf_op jit(solution)/shard_map/psum | solution.py:1090
  386.8 2.6 slice.89
  390.2 3.9 fusion.1
  397.7 5.6 %outputs.1 = bf16[512,768]{1,0:T(8,128)(2,1)} custom-call(s32[1]{0:T(128)} %bitcast.1.nv_ref, bf16[2048,768]{1,0:T(8,128)(2,1)} %bitcast.13.came_ref, f32[8,512]{1,0:T(8,128)} %get-tuple-element.54.slots_ref, f32[512,768]{1,0:T(8,128)} %get-tuple-element.60.hidden_ref), custom_call_target="tpu_custom_call" | custom-call | flops 1610612736 | bytes 8388608 | tf_op jit(solution)/shard_map/outputs/pallas_call | solution.py:55
  (91 shorter events, 29.8 us)
Async XLA Ops:
  8.5 27.8 %collective-permute-start.2 = (bf16[768,768]{1,0:T(8,128)(2,1)S(1)}, bf16[768,768]{1,0:T(8,128)(2,1)S(1)}, u32[]{:S(2)}, u32[]{:S(2)}) collective-permute-start(bf16[768,768]{1,0:T(8,128)(2,1)S(1)} %pad_maximum_fusion.1), channel_id=1, source_target_pairs={{0,2},{1,3},{2,0},{3,1},{4,6},{5,7},{6,4},{7,5},{8,10},{9,11},{10,... | collective-permute-start | bytes 3538952 | tf_op jit(solution)/shard_map/ppermute | solution.py:955
  16.1 92.6 %all-to-all-start = ((bf16[8,256,768]{2,1,0:T(8,128)(2,1)}), bf16[8,256,768]{2,1,0:T(8,128)(2,1)}, u32[]{:S(2)}, u32[]{:S(2)}) async-start(bf16[8,256,768]{2,1,0:T(8,128)(2,1)} %bitcast.35), calls=%async_computation | async-start | bytes 6291456 | tf_op jit(solution)/shard_map/all_to_all | solution.py:976
  22.5 15.3 %copy-start.1 = (bf16[512,768]{1,0:T(8,128)(2,1)S(1)}, bf16[512,768]{1,0:T(8,128)(2,1)}, u32[]{:S(2)}) copy-start(bf16[512,768]{1,0:T(8,128)(2,1)} %x_ref.3) | copy-start | bytes 2359300
  22.5 15.3 %copy-start.9 = (f32[32,3]{0,1:T(4,128)S(1)}, f32[32,3]{0,1:T(4,128)}, u32[]{:S(2)}) copy-start(f32[32,3]{0,1:T(4,128)} %param.18) | copy-start | bytes 1156
  22.6 15.9 %copy-start.7 = (f32[768]{0:T(1024)S(1)}, f32[768]{0:T(1024)}, u32[]{:S(2)}) copy-start(f32[768]{0:T(1024)} %param.15) | copy-start | bytes 9220
  36.3 67.1 %collective-permute-start.3 = (bf16[1536,768]{1,0:T(8,128)(2,1)}, bf16[1536,768]{1,0:T(8,128)(2,1)}, u32[]{:S(2)}, u32[]{:S(2)}) collective-permute-start(bf16[1536,768]{1,0:T(8,128)(2,1)} %pad_maximum_fusion.w0), channel_id=1, source_target_pairs={{0,2},{1,3},{2,0},{3,1},{4,6},{5,7},{6,4},{7,5},{8,10},{9,11},{10,... | collective-permute-start | bytes 7077896 | tf_op jit(solution)/shard_map/ppermute | solution.py:955
  37.8 2.4 collective-permute-start.1
  37.9 51.2 %collective-permute-start = (f32[32,3]{1,0:T(8,128)S(1)}, f32[32,3]{1,0:T(8,128)S(1)}, u32[]{:S(2)}, u32[]{:S(2)}) collective-permute-start(f32[32,3]{1,0:T(8,128)S(1)} %copy.27.table_ref), channel_id=1, source_target_pairs={{0,2},{1,3},{2,0},{3,1},{4,6},{5,7},{6,4},{7,5},{8,10},{9,11},{10,... | collective-permute-start | bytes 1160 | tf_op jit(solution)/shard_map/ppermute | solution.py:955
  89.7 13.8 %copy-start.8 = (f32[768]{0:T(1024)S(1)}, f32[768]{0:T(1024)}, u32[]{:S(2)}) copy-start(f32[768]{0:T(1024)} %param.19) | copy-start | bytes 9220
  89.7 14.5 %copy-start.5 = (bf16[768,8]{0,1:T(8,128)(2,1)S(1)}, bf16[768,8]{0,1:T(8,128)(2,1)}, u32[]{:S(2)}) copy-start(bf16[768,8]{0,1:T(8,128)(2,1)} %param.20) | copy-start | bytes 36868
  99.8 3.6 collective-permute-start.4
  99.8 8.9 %collective-permute-start.5 = (bf16[1536,768]{1,0:T(8,128)(2,1)}, bf16[1536,768]{1,0:T(8,128)(2,1)}, u32[]{:S(2)}, u32[]{:S(2)}) collective-permute-start(bf16[1536,768]{1,0:T(8,128)(2,1)} %pad_maximum_fusion.w0), channel_id=1, source_target_pairs={{0,1},{1,0},{2,3},{3,2},{4,5},{5,4},{6,7},{7,6},{8,9},{9,8},{10,11... | collective-permute-start | bytes 7077896 | tf_op jit(solution)/shard_map/ppermute | solution.py:955
  103.4 5.8 %collective-permute-start.6 = (bf16[1536,768]{1,0:T(8,128)(2,1)}, bf16[1536,768]{1,0:T(8,128)(2,1)}, u32[]{:S(2)}, u32[]{:S(2)}) collective-permute-start(bf16[1536,768]{1,0:T(8,128)(2,1)} %collective-permute-done.3.w2), channel_id=1, source_target_pairs={{0,1},{1,0},{2,3},{3,2},{4,5},{5,4},{6,7},{7,6},{8,9},{9,8},{10,11... | collective-permute-start | bytes 7077896 | tf_op jit(solution)/shard_map/ppermute | solution.py:955
  234.2 32.2 %collective-permute-start.11 = (bf16[1536,768]{1,0:T(8,128)(2,1)S(1)}, bf16[1536,768]{1,0:T(8,128)(2,1)}, u32[]{:S(2)}, u32[]{:S(2)}) collective-permute-start(bf16[1536,768]{1,0:T(8,128)(2,1)S(1)} %get-tuple-element.105), channel_id=1, source_target_pairs={{0,1},{1,0},{2,3},{3,2},{4,5},{5,4},{6,7},{7,6},{8,9},{9,8},{10,11... | collective-permute-start | bytes 7077896 | tf_op jit(solution)/shard_map/ppermute | solution.py:955
  241.1 5.2 %collective-permute-start.7 = (bf16[512,768]{1,0:T(8,128)(2,1)}, bf16[512,768]{1,0:T(8,128)(2,1)S(1)}, u32[]{:S(2)}, u32[]{:S(2)}) collective-permute-start(bf16[512,768]{1,0:T(8,128)(2,1)} %get-tuple-element.65.refs_6_), channel_id=1, source_target_pairs={{0,1},{1,0},{2,3},{3,2},{4,5},{5,4},{6,7},{7,6},{8,9},{9,8},{10,11... | collective-permute-start | bytes 2359304 | tf_op jit(solution)/shard_map/ppermute | solution.py:955
  241.6 156.2 %all-to-all-start.1 = ((bf16[8,256,768]{2,1,0:T(8,128)(2,1)}), bf16[8,256,768]{2,1,0:T(8,128)(2,1)}, u32[]{:S(2)}, u32[]{:S(2)}) async-start(bf16[8,256,768]{2,1,0:T(8,128)(2,1)} %bitcast.12), calls=%async_computation.1 | async-start | bytes 6291456 | tf_op jit(solution)/shard_map/all_to_all | solution.py:976
  246.0 140.8 %all-reduce.2.cloned.1.call-start = ((), (), s32[]{:S(2)}) async-start(), calls=%async_computation.2 | async-start | bytes 2359296 | tf_op jit(solution)/shard_map/psum | solution.py:1090
  246.2 144.0 %collective-permute-start.10 = (bf16[1536,768]{1,0:T(8,128)(2,1)}, bf16[1536,768]{1,0:T(8,128)(2,1)}, u32[]{:S(2)}, u32[]{:S(2)}) collective-permute-start(bf16[1536,768]{1,0:T(8,128)(2,1)} %get-tuple-element.104), channel_id=1, source_target_pairs={{0,1},{1,0},{2,3},{3,2},{4,5},{5,4},{6,7},{7,6},{8,9},{9,8},{10,11... | collective-permute-start | bytes 7077896 | tf_op jit(solution)/shard_map/ppermute | solution.py:955
  264.9 28.8 %collective-permute-start.9 = (bf16[768,768]{1,0:T(8,128)(2,1)S(1)}, bf16[768,768]{1,0:T(8,128)(2,1)S(1)}, u32[]{:S(2)}, u32[]{:S(2)}) collective-permute-start(bf16[768,768]{1,0:T(8,128)(2,1)S(1)} %pad_maximum_fusion.2), channel_id=1, source_target_pairs={{0,2},{1,3},{2,0},{3,1},{4,6},{5,7},{6,4},{7,5},{8,10},{9,11},{10,... | collective-permute-start | bytes 3538952 | tf_op jit(solution)/shard_map/ppermute | solution.py:955
  269.4 120.8 %collective-permute-start.12 = (bf16[1536,768]{1,0:T(8,128)(2,1)S(1)}, bf16[1536,768]{1,0:T(8,128)(2,1)}, u32[]{:S(2)}, u32[]{:S(2)}) collective-permute-start(bf16[1536,768]{1,0:T(8,128)(2,1)S(1)} %fusion), channel_id=1, source_target_pairs={{0,2},{1,3},{2,0},{3,1},{4,6},{5,7},{6,4},{7,5},{8,10},{9,11},{10,... | collective-permute-start | bytes 7077896 | tf_op jit(solution)/shard_map/ppermute | solution.py:955
  287.4 12.1 %collective-permute-start.8 = (bf16[512,768]{1,0:T(8,128)(2,1)}, bf16[512,768]{1,0:T(8,128)(2,1)S(1)}, u32[]{:S(2)}, u32[]{:S(2)}) collective-permute-start(bf16[512,768]{1,0:T(8,128)(2,1)} %get-tuple-element.71), channel_id=1, source_target_pairs={{0,1},{1,0},{2,3},{3,2},{4,5},{5,4},{6,7},{7,6},{8,9},{9,8},{10,11... | collective-permute-start | bytes 2359304 | tf_op jit(solution)/shard_map/ppermute | solution.py:955
  293.7 5.5 %copy-start.11 = (f32[8,128]{1,0:T(8,128)S(1)}, f32[8,128]{1,0:T(8,128)}, u32[]{:S(2)}) copy-start(f32[8,128]{1,0:T(8,128)} %get-tuple-element.77) | copy-start | bytes 12292
  293.7 5.6 %copy-start.10 = (f32[8,128]{1,0:T(8,128)S(1)}, f32[8,128]{1,0:T(8,128)}, u32[]{:S(2)}) copy-start(f32[8,128]{1,0:T(8,128)} %get-tuple-element.78) | copy-start | bytes 12292
  300.4 4.8 %copy-start.4 = (f32[6144]{0:T(1024)S(1)}, f32[6144]{0:T(1024)}, u32[]{:S(2)}) copy-start(f32[6144]{0:T(1024)} %reshape.111) | copy-start | bytes 73732
  (8 other events, 12.8 us)
Sparse Core Ops, SparseCore 0:
  296.8 89.9 all-reduce.1
